TPU v7x, 512 devices: a whole 4x8x8 slice. The times are simulated.
512 devices in a mesh: lat: 32 (over x, y), chan: 16 (over z, core).
Axes of the slice: x: 4, y: 8, z: 8, core: 2. Of those that a mesh axis runs over, the one named last changes fastest.
Arguments:
- grid_field: bfloat16 [512, 128, 1440], P('lat', 'chan'), may hold values from -6 to 6
- legendre: bfloat16 [512, 192, 385], P(None, 'lat'), may hold values from -0.25 to 0.25
- mix_weight: bfloat16 [2, 128, 128], P(None, 'chan'), may hold values from -0.375 to 0.375
- pair_order: int32 [192], replicated, may hold values from 0 to 191, each once
Outputs:
- mixed_coeffs: bfloat16 [192, 2, 128, 385], P('lat', None, 'chan')
Inputs may be any that keep to these rules, and one draw needn't show every extreme that they name: `pair_order`: each pair 0 to 191 stands at exactly one position.
All inputs are finite; a program needn't handle non-finite values.
Results may differ from a plain program's by a relative error of at most 0.025.
Values may be sent and summed in bfloat16 or wider, within the bound.
A program may use at most 64 MiB of HBM per device.

v0:
```python
import math

import jax
import jax.numpy as jnp
from jax import lax
from jax.sharding import PartitionSpec as P


def fourier_tables(lon_count, order_count):
    orders = lax.broadcasted_iota(jnp.int32, (lon_count, order_count), 1)
    columns = lax.broadcasted_iota(jnp.int32, (lon_count, order_count), 0)
    phases = 2.0 * math.pi / lon_count * (orders * columns % lon_count).astype(jnp.float32)
    return (jnp.cos(phases).astype(jnp.bfloat16), jnp.sin(phases).astype(jnp.bfloat16))


def body(grid_field, legendre, mix_weight, pair_order):
    lat_rows, chan_cols, lon_count = grid_field.shape
    slot_count = legendre.shape[2]
    order_count = slot_count - 1
    pair_total = pair_order.shape[0]
    cosine, sine_table = fourier_tables(lon_count, order_count)
    flat_field = grid_field.reshape(lat_rows * chan_cols, lon_count)
    real_part = jnp.dot(flat_field, cosine, preferred_element_type=jnp.float32) / math.sqrt(
        lon_count
    )
    imag_part = -jnp.dot(flat_field, sine_table, preferred_element_type=jnp.float32) / math.sqrt(
        lon_count
    )
    spectrum = jnp.stack(
        [
            real_part.reshape(lat_rows, chan_cols, order_count),
            imag_part.reshape(lat_rows, chan_cols, order_count),
        ],
        axis=1,
    ).astype(jnp.bfloat16)
    first_order = jnp.take(spectrum, pair_order, axis=3)
    second_order = jnp.take(spectrum, order_count - 1 - pair_order, axis=3)
    slot_ids = lax.broadcasted_iota(jnp.int32, (pair_total, slot_count), 1)
    slot_mask = slot_ids < (order_count - pair_order)[:, None]
    band_table = lax.all_to_all(legendre, "lat", split_axis=0, concat_axis=1, tiled=True)
    with_first = jnp.einsum(
        "lkn,lrck->krcn", band_table, first_order, preferred_element_type=jnp.float32
    )
    with_second = jnp.einsum(
        "lkn,lrck->krcn", band_table, second_order, preferred_element_type=jnp.float32
    )
    summed = lax.psum_scatter(
        jnp.where(slot_mask[:, None, None, :], with_first, with_second).astype(jnp.bfloat16),
        "lat",
        scatter_dimension=0,
        tiled=True,
    )
    pieces = lax.all_gather(summed, "chan", axis=2, tiled=True)
    real_in = pieces[:, 0]
    imag_in = pieces[:, 1]
    real_out = jnp.einsum(
        "oc,kcn->kon", mix_weight[0], real_in, preferred_element_type=jnp.float32
    ) - jnp.einsum("oc,kcn->kon", mix_weight[1], imag_in, preferred_element_type=jnp.float32)
    imag_out = jnp.einsum(
        "oc,kcn->kon", mix_weight[0], imag_in, preferred_element_type=jnp.float32
    ) + jnp.einsum("oc,kcn->kon", mix_weight[1], real_in, preferred_element_type=jnp.float32)
    mixed = jnp.stack([real_out, imag_out], axis=1)
    return mixed.astype(jnp.bfloat16)


def solution(mesh):
    return jax.shard_map(
        body,
        mesh=mesh,
        in_specs=(P("lat", "chan", None), P(None, "lat", None), P(None, "chan", None), P()),
        out_specs=P("lat", None, "chan", None),
        check_vma=False,
    )
```

profile of v0, /device:TPU:1, one launch (start us, length us, event | category | flops | bytes accessed | tf_op | source)
XLA Modules:
  0.0 409.9 jit_solution(13184104640811517915)
XLA Ops:
  6.5 0.0 copy-start
  6.5 7.8 %copy.34 = bf16[512,6,385]{2,1,0:T(8,128)(2,1)} copy(bf16[512,6,385]{0,2,1:T(8,128)(2,1)} %param.7) | data formatting | bytes 4730880 | tf_op args[1]
  14.3 10.6 %all-to-all-start = ((bf16[512,6,385]{2,1,0:T(8,128)(2,1)}), bf16[512,6,385]{2,1,0:T(8,128)(2,1)}, u32[]{:S(2)}, u32[]{:S(2)}) async-start(bf16[512,6,385]{2,1,0:T(8,128)(2,1)} %copy.34), calls=%async_computation | async-start | bytes 8388608 | tf_op jit(solution)/shard_map/all_to_all | solution.py:40
  25.0 0.0 reduce-scatter.2.cloned.1.call-start
  25.0 0.0 copy-done
  25.0 9.1 %fusion.9 = bf16[16,1,8,384]{3,2,0,1:T(8,128)(2,1)S(1)} fusion(bf16[16,8,1440]{2,1,0:T(8,128)(2,1)S(1)} %copy-done), kind=kOutput, calls=%fused_computation.19 | convolution fusion | flops 147234816 | bytes 466944 | tf_op jit(solution)/shard_map/dot_general | solution.py:26
  34.2 0.5 copy.33
  34.7 0.0 copy-start.1
  34.7 9.1 %fusion.8 = bf16[16,1,8,384]{3,2,0,1:T(8,128)(2,1)S(1)} fusion(bf16[16,8,1440]{2,1,0:T(8,128)(2,1)S(1)} %copy-done), kind=kOutput, calls=%fused_computation.18 | convolution fusion | flops 147185664 | bytes 466944 | tf_op jit(solution)/shard_map/dot_general | solution.py:23
  43.8 0.5 copy.32
  44.3 0.0 copy-done.1
  44.3 0.4 pad_maximum_fusion
  44.7 0.9 gather_fusion
  45.6 0.9 gather_fusion.1
  46.4 0.1 iota_compare_fusion
  46.6 71.0 %all-to-all-done = bf16[512,6,385]{2,1,0:T(8,128)(2,1)} async-done(((bf16[512,6,385]{2,1,0:T(8,128)(2,1)}), bf16[512,6,385]{2,1,0:T(8,128)(2,1)}, u32[]{:S(2)}, u32[]{:S(2)}) %all-to-all-start) | async-done | bytes 2365472 | tf_op jit(solution)/shard_map/all_to_all | solution.py:40
  117.5 3.6 copy.36
  121.1 1.0 fusion.19
  122.1 2.6 select_convert_fusion
  124.7 0.0 copy-start.3
  124.7 0.0 reduce-scatter.2.cloned.1.call-update
  124.7 0.0 all-gather.2.cloned.1.call-start
  124.8 224.4 %reduce-scatter.2.cloned.1.call-done = bf16[6,2,8,385]{3,2,1,0:T(8,128)(2,1)} async-done(((bf16[192,2,8,385]{3,2,1,0:T(8,128)(2,1)}), bf16[6,2,8,385]{3,2,1,0:T(8,128)(2,1)}) %reduce-scatter.2.cloned.1.call-update) | async-done | bytes 73936 | tf_op jit(solution)/shard_map/reduce_scatter | solution.py:47
  349.2 0.0 all-gather.2.cloned.1.call-update
  349.2 48.8 %all-gather.2.cloned.1.call-done = bf16[6,2,128,385]{3,2,1,0:T(8,128)(2,1)} async-done(((bf16[6,2,8,385]{3,2,1,0:T(8,128)(2,1)}), bf16[6,2,128,385]{3,2,1,0:T(8,128)(2,1)}) %all-gather.2.cloned.1.call-update) | async-done | bytes 1182736 | tf_op jit(solution)/shard_map/all_gather | solution.py:53
  398.0 0.0 copy-done.3
  398.0 0.0 copy-start.2
  398.0 1.5 fusion.26
  399.5 1.3 fusion.25
  400.8 1.4 fusion.12
  402.2 0.0 copy-done.2
  402.2 0.2 fusion.13
  402.4 0.6 copy.41
  (4 shorter events, 0.0 us)
Async XLA Ops:
  6.5 18.5 %copy-start = (bf16[16,8,1440]{2,1,0:T(8,128)(2,1)S(1)}, bf16[16,8,1440]{2,1,0:T(8,128)(2,1)}, u32[]{:S(2)}) copy-start(bf16[16,8,1440]{2,1,0:T(8,128)(2,1)} %param.6) | copy-start | bytes 1105924
  14.3 103.2 %all-to-all-start = ((bf16[512,6,385]{2,1,0:T(8,128)(2,1)}), bf16[512,6,385]{2,1,0:T(8,128)(2,1)}, u32[]{:S(2)}, u32[]{:S(2)}) async-start(bf16[512,6,385]{2,1,0:T(8,128)(2,1)} %copy.34), calls=%async_computation | async-start | bytes 8388608 | tf_op jit(solution)/shard_map/all_to_all | solution.py:40
  25.0 324.3 %reduce-scatter.2.cloned.1.call-start = ((), (), s32[]{:S(2)}) async-start(), calls=%async_computation.2 | async-start | bytes 3244032 | tf_op jit(solution)/shard_map/reduce_scatter | solution.py:47
  34.7 9.6 %copy-start.1 = (s32[192]{0:T(256)S(1)}, s32[192]{0:T(256)}, u32[]{:S(2)}) copy-start(s32[192]{0:T(256)} %param.9) | copy-start | bytes 2308
  124.7 273.3 %copy-start.3 = (bf16[2,8,128]{2,1,0:T(8,128)(2,1)S(1)}, bf16[2,8,128]{2,1,0:T(8,128)(2,1)}, u32[]{:S(2)}) copy-start(bf16[2,8,128]{2,1,0:T(8,128)(2,1)} %param.8) | copy-start | bytes 12292
  124.7 273.3 %all-gather.2.cloned.1.call-start = ((), (), s32[]{:S(2)}) async-start(), calls=%async_computation.3 | async-start | bytes 1671168 | tf_op jit(solution)/shard_map/all_gather | solution.py:53
  398.0 4.2 %copy-start.2 = (bf16[6,2,128,385]{3,2,1,0:T(8,128)(2,1)S(1)}, bf16[6,2,128,385]{3,2,1,0:T(8,128)(2,1)}, u32[]{:S(2)}) copy-start(bf16[6,2,128,385]{3,2,1,0:T(8,128)(2,1)} %all-gather.2.cloned.1.call-done) | copy-start | bytes 3548164
Sparse Core Ops, SparseCore 0:
  124.8 224.3 reduce-scatter.1
  351.6 46.4 all-gather.1
where the time goes:
time: 410 us
  waiting for transfers between devices  344 us (84%)
  matrix products  26.2 us (6%)
  local copies, waits for them, and re-layouts  14.8 us (4%)
  between operations  13.5 us (3%)
  starting transfers between devices  10.7 us (3%)
    reduce_scatter x1, waiting for transfers between devices, body(): lax.psum_scatter(jnp.where(slot_mask[:, None, None, :], with_first, with_...  224 us
    all_to_all x1, waiting for transfers between devices, body(): lax.all_to_all(legendre, 'lat', split_axis=0, concat_axis=1, tiled=True)  71 us
    all_gather x1, waiting for transfers between devices, body(): pieces = lax.all_gather(summed, 'chan', axis=2, tiled=True)  48.8 us
    all_to_all x1, starting transfers between devices, body(): lax.all_to_all(legendre, 'lat', split_axis=0, concat_axis=1, tiled=True)  10.6 us
    dot_general x1, matrix products, body(): jnp.dot(flat_field, sine_table, preferred_element_type=jnp.float32)  9.13 us
    dot_general x1, matrix products, body(): jnp.dot(flat_field, cosine, preferred_element_type=jnp.float32)  9.07 us
  transfers between devices with their start and end apart: 3, of which 3 were waited for; matrix products, arithmetic and copies ran while one was open for 5% of the time, Pallas kernels for 0%

commit v1 on v0

v1 whole, which is shorter than its diff:
```python
import math

import jax
import jax.numpy as jnp
import ml_dtypes
import numpy as np
from jax import lax
from jax.sharding import PartitionSpec as P


def fourier_table(lon_count, order_count):
    orders = np.arange(order_count, dtype=np.int32)[None, :]
    columns = np.arange(lon_count, dtype=np.int32)[:, None]
    phases = np.float32(2.0 * math.pi / lon_count) * ((orders * columns) % lon_count).astype(np.float32)
    table = np.concatenate([np.cos(phases), -np.sin(phases)], axis=1)
    return table.astype(ml_dtypes.bfloat16)


def body(grid_field, legendre, mix_weight, pair_order):
    lat_rows, chan_cols, lon_count = grid_field.shape
    pair_rows, slot_count = legendre.shape[1:]
    order_count = slot_count - 1
    table = jnp.asarray(fourier_table(lon_count, order_count))
    flat_field = grid_field.reshape(lat_rows * chan_cols, lon_count)
    spectrum = (
        jnp.dot(flat_field, table, preferred_element_type=jnp.float32) / math.sqrt(lon_count)
    ).astype(jnp.bfloat16)
    spectrum = spectrum.reshape(lat_rows, chan_cols, 2, order_count)
    both = jnp.stack([pair_order, order_count - 1 - pair_order], axis=1).reshape(-1)
    picked = jnp.take(spectrum, both, axis=3)
    moved = lax.all_to_all(picked, "lat", split_axis=3, concat_axis=0, tiled=True)
    lat_count = moved.shape[0]
    moved = moved.reshape(lat_count, chan_cols, 2, pair_rows, 2)
    mine = lax.dynamic_slice_in_dim(pair_order, lax.axis_index("lat") * pair_rows, pair_rows)
    slot_ids = lax.broadcasted_iota(jnp.int32, (pair_rows, slot_count), 1)
    slot_mask = slot_ids < (order_count - mine)[:, None]
    sums = jnp.einsum("tkn,tcrkh->khrcn", legendre, moved, preferred_element_type=jnp.float32)
    summed = jnp.where(slot_mask[:, None, None, :], sums[:, 0], sums[:, 1]).astype(jnp.bfloat16)
    pieces = lax.all_gather(summed, "chan", axis=2, tiled=True)
    channels = pieces.shape[2]
    w_real, w_imag = mix_weight[0], mix_weight[1]
    weights = jnp.stack(
        [jnp.stack([w_real, -w_imag], axis=1), jnp.stack([w_imag, w_real], axis=1)], axis=0
    ).reshape(2 * chan_cols, 2 * channels)
    mixed = jnp.einsum(
        "oc,kcn->kon",
        weights,
        pieces.reshape(pair_rows, 2 * channels, slot_count),
        preferred_element_type=jnp.float32,
    )
    return mixed.reshape(pair_rows, 2, chan_cols, slot_count).astype(jnp.bfloat16)


def solution(mesh):
    return jax.shard_map(
        body,
        mesh=mesh,
        in_specs=(P("lat", "chan", None), P(None, "lat", None), P(None, "chan", None), P()),
        out_specs=P("lat", None, "chan", None),
        check_vma=False,
    )
```

time: 410 us -> 108 us (0.26)
  waiting for transfers between devices: 344 us -> 53.3 us
  matrix products: 26.2 us -> 5.62 us
  other arithmetic: 0.52 us -> 5.67 us
  local copies, waits for them, and re-layouts: 14.8 us -> 19.4 us
    reduce_scatter x1 -> x0, waiting for transfers between devices: 224 us -> none  [body(): lax.psum_scatter(jnp.where(slot_mask[:, None, None, :], with_first, with_...]
    all_to_all x1, waiting for transfers between devices: 71 us -> 9.19 us  [body(): lax.all_to_all(picked, 'lat', split_axis=3, concat_axis=0, tiled=True)]
    dot_general x8 -> x3, matrix products: 26.2 us -> 5.62 us  [the longest x1 2.49 us: body(): jnp.dot(flat_field, table, preferred_element_type=jnp.float32)]
    reshape x0 -> x5, local copies, waits for them, and re-layouts: none -> 5.99 us  [the longest x1 3.56 us: body(): moved = moved.reshape(lat_count, chan_cols, 2, pair_rows, 2)]
    all_gather x1, waiting for transfers between devices: 48.8 us -> 44.1 us  [body(): pieces = lax.all_gather(summed, 'chan', axis=2, tiled=True)]
  transfers between devices with their start and end apart: 3 -> 2, of which waited for: 3 -> 2; matrix products, arithmetic and copies ran while one was open for 5% -> 0% of each run, Pallas kernels for 0% -> 0%
where the time goes in v1:
time: 108 us
  waiting for transfers between devices  53.3 us (49%)
  local copies, waits for them, and re-layouts  19.4 us (18%)
  between operations  13.5 us (12%)
  starting transfers between devices  10.5 us (10%)
  other arithmetic  5.67 us (5%)
  matrix products  5.62 us (5%)
    all_gather x1, waiting for transfers between devices, body(): pieces = lax.all_gather(summed, 'chan', axis=2, tiled=True)  44.1 us
    all_to_all x1, starting transfers between devices, body(): lax.all_to_all(picked, 'lat', split_axis=3, concat_axis=0, tiled=True)  10.5 us
    all_to_all x1, waiting for transfers between devices, body(): lax.all_to_all(picked, 'lat', split_axis=3, concat_axis=0, tiled=True)  9.19 us
    unnamed x8, local copies, waits for them, and re-layouts  5.95 us
    gather x1, local copies, waits for them, and re-layouts, body(): picked = jnp.take(spectrum, both, axis=3)  3.61 us
    all_to_all x1, local copies, waits for them, and re-layouts, body(): lax.all_to_all(picked, 'lat', split_axis=3, concat_axis=0, tiled=True)  3.58 us
    reshape x1, local copies, waits for them, and re-layouts, body(): moved = moved.reshape(lat_count, chan_cols, 2, pair_rows, 2)  3.56 us
    unnamed x1, other arithmetic  3.29 us
  transfers between devices with their start and end apart: 2, of which 2 were waited for; matrix products, arithmetic and copies ran while one was open for 0% of the time, Pallas kernels for 0%

profile of v1, /device:TPU:1, one launch (start us, length us, event | category | flops | bytes accessed | tf_op | source)
XLA Modules:
  0.0 108.1 jit_solution(17065313400028907341)
XLA Ops:
  6.5 0.0 copy-start
  6.5 0.8 broadcast_subtract_fusion
  7.4 0.7 pad_add_fusion
  8.1 0.1 copy.15
  8.2 0.1 reshape.85
  8.3 0.1 reshape.82
  8.5 2.5 %fusion.6 = bf16[128,768]{0,1:T(8,128)(2,1)S(1)} fusion(bf16[1440,768]{1,0:T(8,128)(2,1)} %constant.34.clone, bf16[16,8,1440]{2,1,0:T(8,128)(2,1)} %param.5), kind=kOutput, calls=%fused_computation.7 | convolution fusion | flops 283312128 | bytes 2777088 | tf_op jit(solution)/shard_map/dot_general | solution.py:26
  11.0 0.1 copy.16
  11.2 0.1 reshape.84
  11.2 2.1 %copy.18 = bf16[16,8,2,384]{0,1,3,2:T(8,128)(2,1)} copy(bf16[16,8,2,384]{3,2,1,0:T(2,128)(2,1)S(1)} %reshape.84) | data formatting | bytes 393216 | tf_op jit(solution)/shard_map/reshape | solution.py:28
  13.3 3.6 %gather_fusion = bf16[384,16,8,2]{1,2,3,0:T(8,128)(2,1)} fusion(bf16[16,8,2,384]{0,1,3,2:T(8,128)(2,1)} %copy.18, s32[1024]{0:T(1024)S(1)} %pad_clamp_fusion), kind=kCustom, calls=%fused_computation | custom fusion | bytes 394752 | tf_op jit(solution)/shard_map/jit(_take)/gather | solution.py:30
  16.9 3.3 %fusion.17 = bf16[384,2,8,16]{3,2,1,0:T(8,128)(2,1)} fusion(bf16[384,16,8,2]{1,2,3,0:T(8,128)(2,1)} %gather_fusion, pred[384]{0:T(512)(128)(4,1)S(1)} %compare_and_fusion), kind=kLoop, calls=%fused_computation.34 | loop fusion | flops 98304 | bytes 393600
  20.2 0.0 copy-start.2
  20.2 3.7 %reshape.100 = bf16[32,2,1536]{2,1,0:T(2,128)(2,1)} reshape(bf16[384,2,8,16]{3,2,1,0:T(8,128)(2,1)} %fusion.17) | data formatting | bytes 393216
  24.0 10.5 %all-to-all-start = ((bf16[32,2,1536]{2,1,0:T(2,128)(2,1)}), bf16[32,2,1536]{2,1,0:T(2,128)(2,1)S(1)}, u32[]{:S(2)}, u32[]{:S(2)}) async-start(bf16[32,2,1536]{2,1,0:T(2,128)(2,1)} %reshape.100), calls=%async_computation | async-start | bytes 393216 | tf_op jit(solution)/shard_map/all_to_all | solution.py:31
  34.5 0.0 all-gather.2.cloned.1.call-start
  34.5 0.0 copy-done.2
  34.5 0.1 dynamic-slice_subtract_fusion
  34.6 0.1 iota_compare_fusion
  34.7 9.2 %all-to-all-done = bf16[32,2,1536]{2,1,0:T(2,128)(2,1)S(1)} async-done(((bf16[32,2,1536]{2,1,0:T(2,128)(2,1)}), bf16[32,2,1536]{2,1,0:T(2,128)(2,1)S(1)}, u32[]{:S(2)}, u32[]{:S(2)}) %all-to-all-start) | async-done | bytes 196640 | tf_op jit(solution)/shard_map/all_to_all | solution.py:31
  43.9 2.2 %reshape.101 = bf16[384,2,8,16]{3,2,1,0:T(8,128)(2,1)} reshape(bf16[32,2,1536]{2,1,0:T(2,128)(2,1)S(1)} %all-to-all-done) | data formatting | bytes 393216
  46.1 3.6 %copy.20 = bf16[32,16,8,2,12]{1,0,2,4,3:T(8,128)(2,1)} copy(bf16[32,16,8,2,12]{1,2,3,4,0:T(8,128)(2,1)} %bitcast.65) | data formatting | bytes 393216 | tf_op jit(solution)/shard_map/all_to_all | solution.py:31
  49.7 3.6 %reshape.86 = bf16[512,8,2,6,2]{0,1,4,3,2:T(8,128)(2,1)S(1)} reshape(bf16[32,16,8,2,12]{1,0,2,4,3:T(8,128)(2,1)} %copy.20) | data formatting | bytes 393216 | tf_op jit(solution)/shard_map/reshape | solution.py:33
  53.2 0.0 copy-done
  53.2 0.0 copy-start.1
  53.2 0.8 fusion.2
  54.0 0.7 fusion.10
  54.7 0.0 all-gather.2.cloned.1.call-update
  54.7 0.0 copy-done.1
  54.8 44.1 %all-gather.2.cloned.1.call-done = bf16[6,2,128,385]{3,2,1,0:T(8,128)(2,1)} async-done(((bf16[6,2,8,385]{3,2,1,0:T(8,128)(2,1)}), bf16[6,2,128,385]{3,2,1,0:T(8,128)(2,1)}) %all-gather.2.cloned.1.call-update) | async-done | bytes 1182736 | tf_op jit(solution)/shard_map/all_gather | solution.py:39
  98.9 2.4 %fusion.7 = bf16[6,2,8,385]{3,2,1,0:T(8,128)(2,1)} fusion(bf16[6,256,385]{2,1,0:T(8,128)(2,1)} %bitcast.66, bf16[1,8,2,128]{3,1,2,0:T(8,128)(2,1)S(1)} %get-tuple-element.8, bf16[1,8,2,128]{3,1,2,0:T(8,128)(2,1)S(1)} %get-tuple-element.7), kind=kOutput, calls=%fused_computation.9 | convolution fusion | flops 18964576 | bytes 1264832 | tf_op jit(solution)/shard_map/oc,kcn->kon/dot_general | solution.py:45
  (6 shorter events, 0.1 us)
Async XLA Ops:
  6.5 46.7 %copy-start = (bf16[512,6,385]{0,2,1:T(8,128)(2,1)S(1)}, bf16[512,6,385]{0,2,1:T(8,128)(2,1)}, u32[]{:S(2)}) copy-start(bf16[512,6,385]{0,2,1:T(8,128)(2,1)} %param.6) | copy-start | bytes 7096324
  20.2 14.3 %copy-start.2 = (s32[192]{0:T(256)S(1)}, s32[192]{0:T(256)}, u32[]{:S(2)}) copy-start(s32[192]{0:T(256)} %param.8) | copy-start | bytes 2308
  24.0 19.9 %all-to-all-start = ((bf16[32,2,1536]{2,1,0:T(2,128)(2,1)}), bf16[32,2,1536]{2,1,0:T(2,128)(2,1)S(1)}, u32[]{:S(2)}, u32[]{:S(2)}) async-start(bf16[32,2,1536]{2,1,0:T(2,128)(2,1)} %reshape.100), calls=%async_computation | async-start | bytes 393216 | tf_op jit(solution)/shard_map/all_to_all | solution.py:31
  34.5 64.4 %all-gather.2.cloned.1.call-start = ((), (), s32[]{:S(2)}) async-start(), calls=%async_computation.1 | async-start | bytes 1671168 | tf_op jit(solution)/shard_map/all_gather | solution.py:39
  53.2 1.5 %copy-start.1 = (bf16[2,8,128]{2,1,0:T(8,128)(2,1)S(1)}, bf16[2,8,128]{2,1,0:T(8,128)(2,1)}, u32[]{:S(2)}) copy-start(bf16[2,8,128]{2,1,0:T(8,128)(2,1)} %param.7) | copy-start | bytes 12292
Sparse Core Ops, SparseCore 0:
  54.8 44.0 all-gather.1

commit v2 on v1

v2 whole, which is shorter than its diff:
```python
import functools
import math

import jax
import jax.numpy as jnp
import ml_dtypes
import numpy as np
from jax import lax
from jax.experimental import pallas as pl
from jax.experimental.pallas import tpu as pltpu
from jax.sharding import PartitionSpec as P

BF16 = jnp.bfloat16
F32 = jnp.float32
NX, NY, NZ = 4, 8, 8
N_LAT, N_CHAN = NX * NY, 2 * NZ
LAT, CH, NLON = 16, 8, 1440
ORDERS, SLOTS, PAIRS, MINE = 384, 385, 192, 6
ROWS = 4 * MINE
UNITS = 19
EXTRA = (0, 6, 10)
MESH = pl.DeviceIdType.MESH
NT = (((1,), (1,)), ((), ()))


def fourier_table():
    orders = np.arange(ORDERS, dtype=np.int32)[:, None]
    columns = np.arange(NLON, dtype=np.int32)[None, :]
    phases = np.float32(2.0 * math.pi / NLON) * ((orders * columns) % NLON).astype(np.float32)
    return np.concatenate([np.cos(phases), -np.sin(phases)], axis=0).astype(ml_dtypes.bfloat16)


def constants():
    row = np.arange(N_LAT * ROWS)
    part, half, pair = (row // 12) % 2, (row // 6) % 2, (row // ROWS) * MINE + row % MINE
    pick = np.zeros((row.size, PAIRS), np.float32)
    pick[row, pair] = 1 - 2 * half
    base = np.broadcast_to((part * ORDERS + half * (ORDERS - 1))[:, None], (row.size, 128))
    s, t, c = np.meshgrid(np.arange(8), np.arange(LAT), np.arange(CH), indexing="ij")
    regroup = np.zeros((1024, 1024), np.float32)
    regroup[(s * 128 + t * CH + c).ravel(), (c * 128 + s * LAT + t).ravel()] = 1
    lane = np.arange(CH * ROWS)
    pair_lane = np.broadcast_to((lane % MINE)[None, :], (8, lane.size)).astype(np.int32)
    k, r, c = np.meshgrid(np.arange(MINE), np.arange(2), np.arange(CH), indexing="ij")
    fold = np.zeros((2, MINE * 16, CH * ROWS), np.float32)
    for half in range(2):
        fold[half, (k * 16 + r * 8 + c).ravel(), (c * ROWS + r * 12 + half * MINE + k).ravel()] = 1
    out_row = np.arange(MINE * 16)
    offset = (np.arange(PAIRS)[None, :] - (out_row // 16)[:, None]).astype(np.int32)
    bf = ml_dtypes.bfloat16
    return (
        fourier_table(),
        pick.astype(bf),
        base.astype(np.float32),
        regroup.astype(bf),
        pair_lane,
        fold.astype(bf),
        offset,
    )


def kernel(
    x_hbm, leg_hbm, mix_hbm, order_hbm, table_hbm, pick_hbm, base_hbm, regroup_hbm, lane_hbm, fold_hbm,
    offset_hbm, out_ref,
    x, leg, order, table, pick, base, regroup, lane, fold, offset,
    send, recv, weights, units, gathered, mixed, back,
    local_sem, lat_send, lat_recv, w_send, w_recv, c_send, c_recv, m_send, m_recv,
):
    li, ci = lax.axis_index("lat"), lax.axis_index("chan")
    lx, ly = li // NY, li % NY
    cz, cc = ci // 2, ci % 2

    def lat_peer(step):
        return lax.rem(lx + step // NY, NX) * NY + lax.rem(ly + step % NY, NY)

    def chan_peer(step):
        return lax.rem(cz + step // 2, NZ) * 2 + lax.rem(cc + step % 2, 2)

    barrier = pltpu.get_barrier_semaphore()

    @pl.loop(1, N_LAT)
    def _(step):
        pl.semaphore_signal(barrier, inc=1, device_id=(lat_peer(step), ci), device_id_type=MESH)

    @pl.loop(1, N_CHAN)
    def _(step):
        pl.semaphore_signal(barrier, inc=1, device_id=(li, chan_peer(step)), device_id_type=MESH)

    loads = [
        pltpu.make_async_copy(src, dst, local_sem.at[i])
        for i, (src, dst) in enumerate(
            [
                (order_hbm, order), (pick_hbm, pick), (base_hbm, base), (x_hbm, x), (table_hbm, table),
                (mix_hbm, weights.at[ci]), (regroup_hbm, regroup), (leg_hbm, leg), (lane_hbm, lane),
                (fold_hbm, fold), (offset_hbm, offset),
            ]
        )
    ]
    for load in loads:
        load.start()
    for load in loads[:3]:
        load.wait()
    order_rows = jnp.broadcast_to(order[...], (128, PAIRS)).astype(F32).astype(BF16)
    key = base[...] + lax.dot_general(pick[...], order_rows, NT, preferred_element_type=F32)
    column = lax.broadcasted_iota(jnp.int32, key.shape, 1).astype(F32)
    place = jnp.concatenate(
        [jnp.where(key == column + 128.0 * b, 1.0, 0.0).astype(BF16) for b in range(2 * ORDERS // 128)],
        axis=1,
    )
    for load in loads[3:5]:
        load.wait()
    spectrum = lax.dot_general(table[...], x[...], NT, preferred_element_type=F32)
    spectrum = (spectrum * (1.0 / math.sqrt(NLON))).astype(BF16)
    placed = jnp.dot(place, spectrum, preferred_element_type=F32)
    send[...] = placed.reshape(N_LAT, ROWS, 128).astype(BF16)

    pl.semaphore_wait(barrier, N_LAT + N_CHAN - 2)

    def lat_copy(dest):
        return pltpu.make_async_remote_copy(
            src_ref=send.at[dest], dst_ref=recv.at[li], send_sem=lat_send.at[dest],
            recv_sem=lat_recv.at[li], device_id=(dest, ci), device_id_type=MESH,
        )

    def lat_arrival(src):
        return pltpu.make_async_remote_copy(
            src_ref=send.at[src], dst_ref=recv.at[src], send_sem=lat_send.at[src],
            recv_sem=lat_recv.at[src], device_id=(src, ci), device_id_type=MESH,
        )

    def w_copy(peer, slot):
        return pltpu.make_async_remote_copy(
            src_ref=weights.at[slot], dst_ref=weights.at[slot], send_sem=w_send.at[peer],
            recv_sem=w_recv.at[slot], device_id=(li, peer), device_id_type=MESH,
        )

    @pl.loop(1, N_LAT)
    def _(step):
        lat_copy(lat_peer(step)).start()

    own = pltpu.make_async_copy(send.at[li], recv.at[li], lat_recv.at[li])
    own.start()
    loads[5].wait()

    @pl.loop(1, N_CHAN)
    def _(step):
        w_copy(chan_peer(step), ci).start()

    for load in loads[6:]:
        load.wait()
    mine = jnp.where(offset[...] == li * MINE, 1.0, 0.0).astype(BF16)
    my_order = lax.dot_general(mine, order_rows, NT, preferred_element_type=F32)
    first = lax.broadcasted_iota(jnp.int32, (MINE * 16, SLOTS), 1).astype(F32) < (
        float(ORDERS) - my_order[:, 0:1]
    )

    own.wait()

    @pl.loop(1, N_LAT)
    def _(step):
        lat_arrival(lat_peer(step)).wait_recv()

    blocks = jnp.concatenate(
        [
            jnp.concatenate([recv[g * 8 + s].astype(F32) for s in range(8)], axis=1)
            for g in range(N_LAT // 8)
        ],
        axis=0,
    ).astype(BF16)
    turned = jnp.dot(blocks, regroup[...], preferred_element_type=F32)
    fields = jnp.concatenate(
        [
            jnp.concatenate(
                [turned[g * ROWS : (g + 1) * ROWS, c * 128 : (c + 1) * 128] for g in range(N_LAT // 8)],
                axis=1,
            )
            for c in range(CH)
        ],
        axis=0,
    ).astype(BF16)
    lanes = jnp.broadcast_to(lane[0:1, :], (SLOTS, CH * ROWS))
    sums = jnp.zeros((SLOTS, CH * ROWS), F32)
    for k in range(MINE):
        one = lax.dot_general(leg[k], fields, NT, preferred_element_type=F32)
        sums = jnp.where(lanes == k, one, sums)
    sums = sums.astype(BF16)
    halves = [lax.dot_general(fold[h], sums, NT, preferred_element_type=F32) for h in range(2)]
    coeffs = jnp.where(first, halves[0], halves[1])
    ends = jnp.zeros((16, 128), F32)
    end_lane = lax.broadcasted_iota(jnp.int32, (16, 128), 1)
    for k in range(MINE):
        piece = coeffs[k * 16 : (k + 1) * 16]
        for b in range(3):
            units[k * 3 + b] = piece[:, b * 128 : (b + 1) * 128].astype(BF16)
        ends = jnp.where(end_lane == k, jnp.broadcast_to(piece[:, ORDERS:], (16, 128)), ends)
    units[UNITS - 1] = ends.astype(BF16)

    def unit_copy(unit, slot, peer, src):
        return pltpu.make_async_remote_copy(
            src_ref=units.at[unit], dst_ref=gathered.at[slot, src], send_sem=c_send.at[unit],
            recv_sem=c_recv.at[slot, src], device_id=(li, peer), device_id_type=MESH,
        )

    def back_copy(unit, slot, peer):
        return pltpu.make_async_remote_copy(
            src_ref=mixed.at[slot, peer], dst_ref=back.at[unit], send_sem=m_send.at[slot, peer],
            recv_sem=m_recv.at[unit], device_id=(li, peer), device_id_type=MESH,
        )

    def keep_unit(unit, slot):
        return pltpu.make_async_copy(units.at[unit], gathered.at[slot, ci], c_recv.at[slot, ci])

    def keep_back(unit, slot):
        return pltpu.make_async_copy(mixed.at[slot, ci], back.at[unit], m_recv.at[unit])

    for e, owner in enumerate(EXTRA):

        @pl.when(ci != owner)
        def _():
            unit_copy(16 + e, 1, owner, ci).start()

        @pl.when(ci == owner)
        def _():
            keep_unit(16 + e, 1).start()

    @pl.loop(1, N_CHAN)
    def _(step):
        peer = chan_peer(step)
        unit_copy(peer, 0, peer, ci).start()

    keep_unit(ci, 0).start()

    @pl.loop(1, N_CHAN)
    def _(step):
        peer = chan_peer(step)
        w_copy(peer, peer).wait_recv()

    every = weights[...].astype(F32).reshape(N_CHAN, 2, CH, 128)
    w_real = every[:, 0].reshape(128, 128)
    w_imag = every[:, 1].reshape(128, 128)
    to_real = jnp.concatenate([w_real, -w_imag], axis=1).astype(BF16)
    to_imag = jnp.concatenate([w_imag, w_real], axis=1).astype(BF16)

    def mix(slot, unit):
        keep_unit(unit, slot).wait()

        @pl.loop(1, N_CHAN)
        def _(step):
            peer = chan_peer(step)
            unit_copy(unit, slot, peer, peer).wait_recv()

        both = gathered[slot].astype(F32).reshape(N_CHAN, 2, CH, 128)
        both = jnp.concatenate(
            [both[:, 0].reshape(128, 128), both[:, 1].reshape(128, 128)], axis=0
        ).astype(BF16)
        real = jnp.dot(to_real, both, preferred_element_type=F32).reshape(N_CHAN, CH, 128)
        imag = jnp.dot(to_imag, both, preferred_element_type=F32).reshape(N_CHAN, CH, 128)
        mixed[slot] = jnp.concatenate([real, imag], axis=1).astype(BF16)

        @pl.loop(1, N_CHAN)
        def _(step):
            back_copy(unit, slot, chan_peer(step)).start()

        keep_back(unit, slot).start()

    for e, owner in enumerate(EXTRA):

        @pl.when(ci == owner)
        def _():
            mix(1, 16 + e)

    mix(0, ci)

    @pl.loop(1, N_CHAN)
    def _(step):
        peer = chan_peer(step)
        back_copy(peer, 0, peer).wait_recv()

    keep_back(ci, 0).wait()
    for e, owner in enumerate(EXTRA):

        @pl.when(ci != owner)
        def _():
            back_copy(16 + e, 1, owner).wait_recv()

        @pl.when(ci == owner)
        def _():
            keep_back(16 + e, 1).wait()

    last = back[UNITS - 1].astype(F32)
    for k in range(MINE):
        out_ref[k] = jnp.concatenate(
            [back[k * 3 + b].astype(F32) for b in range(3)] + [last[:, k : k + 1]], axis=1
        ).astype(BF16)

    @pl.loop(1, N_LAT)
    def _(step):
        lat_copy(lat_peer(step)).wait_send()

    @pl.loop(1, N_CHAN)
    def _(step):
        peer = chan_peer(step)
        w_copy(peer, ci).wait_send()
        unit_copy(peer, 0, peer, ci).wait_send()
        back_copy(ci, 0, peer).wait_send()

    for e, owner in enumerate(EXTRA):

        @pl.when(ci != owner)
        def _():
            unit_copy(16 + e, 1, owner, ci).wait_send()

        @pl.when(ci == owner)
        def _():
            @pl.loop(1, N_CHAN)
            def _(step):
                back_copy(16 + e, 1, chan_peer(step)).wait_send()


def body(grid_field, legendre, mix_weight, pair_order):
    any_spec = pl.BlockSpec(memory_space=pl.ANY)
    dma = pltpu.SemaphoreType.DMA
    fixed = [jnp.asarray(c) for c in constants()]
    out = pl.pallas_call(
        kernel,
        out_shape=jax.ShapeDtypeStruct((MINE, 16, SLOTS), BF16),
        in_specs=[any_spec] * 11,
        out_specs=pl.BlockSpec(memory_space=pltpu.VMEM),
        scratch_shapes=[
            pltpu.VMEM((LAT * CH, NLON), BF16),
            pltpu.VMEM((MINE, SLOTS, N_LAT * LAT), BF16),
            pltpu.VMEM((1, PAIRS), jnp.int32),
            pltpu.VMEM((2 * ORDERS, NLON), BF16),
            pltpu.VMEM((N_LAT * ROWS, PAIRS), BF16),
            pltpu.VMEM((N_LAT * ROWS, 128), F32),
            pltpu.VMEM((1024, 1024), BF16),
            pltpu.VMEM((8, CH * ROWS), jnp.int32),
            pltpu.VMEM((2, MINE * 16, CH * ROWS), BF16),
            pltpu.VMEM((MINE * 16, PAIRS), jnp.int32),
            pltpu.VMEM((N_LAT, ROWS, 128), BF16),
            pltpu.VMEM((N_LAT, ROWS, 128), BF16),
            pltpu.VMEM((N_CHAN, 16, 128), BF16),
            pltpu.VMEM((UNITS, 16, 128), BF16),
            pltpu.VMEM((2, N_CHAN, 16, 128), BF16),
            pltpu.VMEM((2, N_CHAN, 16, 128), BF16),
            pltpu.VMEM((UNITS, 16, 128), BF16),
            dma((11,)),
            dma((N_LAT,)),
            dma((N_LAT,)),
            dma((N_CHAN,)),
            dma((N_CHAN,)),
            dma((UNITS,)),
            dma((2, N_CHAN)),
            dma((2, N_CHAN)),
            dma((UNITS,)),
        ],
        compiler_params=pltpu.CompilerParams(
            collective_id=0, has_side_effects=True, vmem_limit_bytes=48 * 1024 * 1024
        ),
    )(
        grid_field.reshape(LAT * CH, NLON),
        jnp.transpose(legendre, (1, 2, 0)),
        mix_weight.reshape(16, 128),
        pair_order.reshape(1, PAIRS),
        *fixed,
    )
    return out.reshape(MINE, 2, CH, SLOTS)


def solution(mesh):
    return jax.shard_map(
        body,
        mesh=mesh,
        in_specs=(P("lat", "chan", None), P(None, "lat", None), P(None, "chan", None), P()),
        out_specs=P("lat", None, "chan", None),
        check_vma=False,
    )
```

time: 108 us -> 52.1 us (0.48)
  waiting for transfers between devices: 53.3 us -> 0 us
  Pallas kernels: 0 us -> 40.9 us
  between operations: 13.5 us -> 0.02 us
  starting transfers between devices: 10.5 us -> 0 us
  local copies, waits for them, and re-layouts: 19.4 us -> 10.7 us
  other arithmetic: 5.67 us -> 0 us
  matrix products: 5.62 us -> 0 us
    all_gather x1 -> x0, waiting for transfers between devices: 44.1 us -> none  [body(): pieces = lax.all_gather(summed, 'chan', axis=2, tiled=True)]
    pallas_call x0 -> x1, Pallas kernels: none -> 40.9 us  [body(): pl.pallas_call(kernel, out_shape=jax.ShapeDtypeStruct((MINE, 16, SLOTS),...]
    all_to_all x1 -> x0, starting transfers between devices: 10.5 us -> none  [body(): lax.all_to_all(picked, 'lat', split_axis=3, concat_axis=0, tiled=True)]
    all_to_all x1 -> x0, waiting for transfers between devices: 9.19 us -> none  [body(): lax.all_to_all(picked, 'lat', split_axis=3, concat_axis=0, tiled=True)]
    reshape x5 -> x0, local copies, waits for them, and re-layouts: 5.99 us -> none  [the longest x1 3.56 us: body(): moved = moved.reshape(lat_count, chan_cols, 2, pair_rows, 2)]
    dot_general x3 -> x0, matrix products: 5.62 us -> none  [the longest x1 2.49 us: body(): jnp.dot(flat_field, table, preferred_element_type=jnp.float32)]
    unnamed x8 -> x21, local copies, waits for them, and re-layouts: 5.95 us -> 10.7 us
    gather x1 -> x0, local copies, waits for them, and re-layouts: 3.61 us -> none  [body(): picked = jnp.take(spectrum, both, axis=3)]
  transfers between devices with their start and end apart: 2 -> 0, of which waited for: 2 -> 0; matrix products, arithmetic and copies ran while one was open for 0% -> 0% of each run, Pallas kernels for 0% -> 0%
where the time goes in v2:
time: 52.1 us; the launch traced here: 51.6 us
  Pallas kernels  40.9 us (79%)
  local copies, waits for them, and re-layouts  10.7 us (21%)
    pallas_call x1, Pallas kernels, body(): pl.pallas_call(kernel, out_shape=jax.ShapeDtypeStruct((MINE, 16, SLOTS),...  40.9 us
    unnamed x21, local copies, waits for them, and re-layouts  10.7 us

profile of v2, /device:TPU:1, one launch (start us, length us, event | category | flops | bytes accessed | tf_op | source)
XLA Modules:
  0.0 51.6 jit_solution(8154539060246988056)
XLA Ops:
  0.0 0.0 copy-start
  0.0 1.7 %copy-done = bf16[768,1440]{1,0:T(8,128)(2,1)S(1)} copy-done((bf16[768,1440]{1,0:T(8,128)(2,1)S(1)}, bf16[768,1440]{1,0:T(8,128)(2,1)}, u32[]{:S(2)}) %copy-start) | copy-done | bytes 2211864
  1.7 0.0 copy-start.1
  1.7 1.6 %copy-done.1 = bf16[1024,1024]{1,0:T(8,128)(2,1)S(1)} copy-done((bf16[1024,1024]{1,0:T(8,128)(2,1)S(1)}, bf16[1024,1024]{1,0:T(8,128)(2,1)}, u32[]{:S(2)}) %copy-start.1) | copy-done | bytes 2097176
  3.3 0.0 copy-start.2
  3.3 1.0 %copy-done.2 = bf16[16,8,1440]{2,1,0:T(8,128)(2,1)S(1)} copy-done((bf16[16,8,1440]{2,1,0:T(8,128)(2,1)S(1)}, bf16[16,8,1440]{2,1,0:T(8,128)(2,1)}, u32[]{:S(2)}) %copy-start.2) | copy-done | bytes 368664
  4.3 0.0 copy-start.3
  4.3 1.0 %copy-done.3 = f32[768,128]{1,0:T(8,128)S(1)} copy-done((f32[768,128]{1,0:T(8,128)S(1)}, f32[768,128]{1,0:T(8,128)}, u32[]{:S(2)}) %copy-start.3) | copy-done | bytes 393240
  5.3 0.0 copy-start.4
  5.3 1.0 %copy-done.4 = bf16[768,192]{1,0:T(8,128)(2,1)S(1)} copy-done((bf16[768,192]{1,0:T(8,128)(2,1)S(1)}, bf16[768,192]{1,0:T(8,128)(2,1)}, u32[]{:S(2)}) %copy-start.4) | copy-done | bytes 294936
  6.2 0.0 copy-start.5
  6.2 0.9 %copy-done.5 = s32[96,192]{1,0:T(8,128)S(1)} copy-done((s32[96,192]{1,0:T(8,128)S(1)}, s32[96,192]{1,0:T(8,128)}, u32[]{:S(2)}) %copy-start.5) | copy-done | bytes 73752
  7.1 0.0 copy-start.6
  7.1 0.9 %copy-done.6 = bf16[2,96,192]{2,1,0:T(8,128)(2,1)S(1)} copy-done((bf16[2,96,192]{2,1,0:T(8,128)(2,1)S(1)}, bf16[2,96,192]{2,1,0:T(8,128)(2,1)}, u32[]{:S(2)}) %copy-start.6) | copy-done | bytes 73752
  8.0 0.0 copy-start.7
  8.0 0.7 %copy-done.7 = s32[8,192]{1,0:T(8,128)S(1)} copy-done((s32[8,192]{1,0:T(8,128)S(1)}, s32[8,192]{1,0:T(8,128)}, u32[]{:S(2)}) %copy-start.7) | copy-done | bytes 6168
  8.7 0.0 copy-start.8
  8.7 0.7 %copy-done.8 = bf16[2,8,128]{2,1,0:T(8,128)(2,1)S(1)} copy-done((bf16[2,8,128]{2,1,0:T(8,128)(2,1)S(1)}, bf16[2,8,128]{2,1,0:T(8,128)(2,1)}, u32[]{:S(2)}) %copy-start.8) | copy-done | bytes 4120
  9.4 0.0 copy-start.9
  9.4 0.7 %copy-done.9 = s32[192]{0:T(256)S(1)} copy-done((s32[192]{0:T(256)S(1)}, s32[192]{0:T(256)}, u32[]{:S(2)}) %copy-start.9) | copy-done | bytes 792
  10.1 40.9 %shard_map.109 = bf16[6,16,385]{2,1,0:T(8,128)(2,1)S(1)} custom-call(bf16[128,1440]{1,0:T(8,128)(2,1)S(1)} %bitcast.6, bf16[6,385,512]{2,1,0:T(8,128)(2,1)} %bitcast.9, bf16[16,128]{1,0:T(8,128)(2,1)S(1)} %bitcast.7, s32[1,192]{1,0:T(1,128)S(1)} %bitcast.8, bf16[768,1440]{1,0:T(8,128)(2,1)S(1)} %copy-done, bf16[768,192]{1,0:T(8,128)(2,1)S(1)} %copy-done.4, ...), custom_call_target="tpu_custom_call" | custom-call | tf_op jit(solution)/shard_map/pallas_call | solution.py:324
  51.0 0.6 %copy.13 = bf16[6,2,8,385]{3,2,1,0:T(8,128)(2,1)} copy(bf16[6,2,8,385]{3,2,1,0:T(8,128)(2,1)S(1)} %bitcast.5) | data formatting | bytes 147840
Async XLA Ops:
  0.0 1.7 %copy-start = (bf16[768,1440]{1,0:T(8,128)(2,1)S(1)}, bf16[768,1440]{1,0:T(8,128)(2,1)}, u32[]{:S(2)}) copy-start(bf16[768,1440]{1,0:T(8,128)(2,1)} %constant.14.clone.table_hbm) | copy-start | bytes 6635524
  1.7 1.6 %copy-start.1 = (bf16[1024,1024]{1,0:T(8,128)(2,1)S(1)}, bf16[1024,1024]{1,0:T(8,128)(2,1)}, u32[]{:S(2)}) copy-start(bf16[1024,1024]{1,0:T(8,128)(2,1)} %constant.17.clone.regroup_hbm) | copy-start | bytes 6291460
  3.3 1.0 %copy-start.2 = (bf16[16,8,1440]{2,1,0:T(8,128)(2,1)S(1)}, bf16[16,8,1440]{2,1,0:T(8,128)(2,1)}, u32[]{:S(2)}) copy-start(bf16[16,8,1440]{2,1,0:T(8,128)(2,1)} %param.11) | copy-start | bytes 1105924
  4.3 1.0 %copy-start.3 = (f32[768,128]{1,0:T(8,128)S(1)}, f32[768,128]{1,0:T(8,128)}, u32[]{:S(2)}) copy-start(f32[768,128]{1,0:T(8,128)} %constant.16.clone.base_hbm) | copy-start | bytes 1179652
  5.3 1.0 %copy-start.4 = (bf16[768,192]{1,0:T(8,128)(2,1)S(1)}, bf16[768,192]{1,0:T(8,128)(2,1)}, u32[]{:S(2)}) copy-start(bf16[768,192]{1,0:T(8,128)(2,1)} %constant.15.clone.pick_hbm) | copy-start | bytes 884740
  6.2 0.9 %copy-start.5 = (s32[96,192]{1,0:T(8,128)S(1)}, s32[96,192]{1,0:T(8,128)}, u32[]{:S(2)}) copy-start(s32[96,192]{1,0:T(8,128)} %constant.20.clone.offset_hbm) | copy-start | bytes 221188
  7.1 0.9 %copy-start.6 = (bf16[2,96,192]{2,1,0:T(8,128)(2,1)S(1)}, bf16[2,96,192]{2,1,0:T(8,128)(2,1)}, u32[]{:S(2)}) copy-start(bf16[2,96,192]{2,1,0:T(8,128)(2,1)} %constant.19.clone.fold_hbm) | copy-start | bytes 221188
  8.0 0.7 %copy-start.7 = (s32[8,192]{1,0:T(8,128)S(1)}, s32[8,192]{1,0:T(8,128)}, u32[]{:S(2)}) copy-start(s32[8,192]{1,0:T(8,128)} %constant.18.clone.lane_hbm) | copy-start | bytes 18436
  8.7 0.7 %copy-start.8 = (bf16[2,8,128]{2,1,0:T(8,128)(2,1)S(1)}, bf16[2,8,128]{2,1,0:T(8,128)(2,1)}, u32[]{:S(2)}) copy-start(bf16[2,8,128]{2,1,0:T(8,128)(2,1)} %param.13) | copy-start | bytes 12292
  9.4 0.7 %copy-start.9 = (s32[192]{0:T(256)S(1)}, s32[192]{0:T(256)}, u32[]{:S(2)}) copy-start(s32[192]{0:T(256)} %param.14) | copy-start | bytes 2308

commit v3 on v2

--- a/solution.py
+++ b/solution.py
@@ -1,4 +1,3 @@
-import functools
 import math
 
 import jax
@@ -70,33 +69,40 @@
     lx, ly = li // NY, li % NY
     cz, cc = ci // 2, ci % 2
 
+    def away(step, ring):
+        return ring // 2 + (1 - 2 * (step % 2)) * ((step + 1) // 2)
+
     def lat_peer(step):
-        return lax.rem(lx + step // NY, NX) * NY + lax.rem(ly + step % NY, NY)
+        dx, dy = away(step % NX, NX), away(step // NX, NY)
+        return lax.rem(lx + dx, NX) * NY + lax.rem(ly + dy, NY)
 
     def chan_peer(step):
-        return lax.rem(cz + step // 2, NZ) * 2 + lax.rem(cc + step % 2, 2)
-
-    barrier = pltpu.get_barrier_semaphore()
-
-    @pl.loop(1, N_LAT)
-    def _(step):
-        pl.semaphore_signal(barrier, inc=1, device_id=(lat_peer(step), ci), device_id_type=MESH)
-
-    @pl.loop(1, N_CHAN)
-    def _(step):
-        pl.semaphore_signal(barrier, inc=1, device_id=(li, chan_peer(step)), device_id_type=MESH)
+        return lax.rem(cz + away(step // 2, NZ), NZ) * 2 + lax.rem(cc + 1 - step % 2, 2)
 
     loads = [
         pltpu.make_async_copy(src, dst, local_sem.at[i])
         for i, (src, dst) in enumerate(
             [
                 (order_hbm, order), (pick_hbm, pick), (base_hbm, base), (x_hbm, x), (table_hbm, table),
-                (mix_hbm, weights.at[ci]), (regroup_hbm, regroup), (leg_hbm, leg), (lane_hbm, lane),
-                (fold_hbm, fold), (offset_hbm, offset),
+                (mix_hbm, weights.at[ci]), (offset_hbm, offset), (lane_hbm, lane), (fold_hbm, fold),
+                (regroup_hbm, regroup), (leg_hbm, leg),
             ]
         )
     ]
-    for load in loads:
+    for load in loads[:5]:
+        load.start()
+
+    barrier = pltpu.get_barrier_semaphore()
+
+    @pl.loop(0, N_LAT - 1)
+    def _(step):
+        pl.semaphore_signal(barrier, inc=1, device_id=(lat_peer(step), ci), device_id_type=MESH)
+
+    @pl.loop(0, N_CHAN - 1)
+    def _(step):
+        pl.semaphore_signal(barrier, inc=1, device_id=(li, chan_peer(step)), device_id_type=MESH)
+
+    for load in loads[5:]:
         load.start()
     for load in loads[:3]:
         load.wait()
@@ -134,7 +140,7 @@
             recv_sem=w_recv.at[slot], device_id=(li, peer), device_id_type=MESH,
         )
 
-    @pl.loop(1, N_LAT)
+    @pl.loop(0, N_LAT - 1)
     def _(step):
         lat_copy(lat_peer(step)).start()
 
@@ -142,7 +148,7 @@
     own.start()
     loads[5].wait()
 
-    @pl.loop(1, N_CHAN)
+    @pl.loop(0, N_CHAN - 1)
     def _(step):
         w_copy(chan_peer(step), ci).start()
 
@@ -156,7 +162,7 @@
 
     own.wait()
 
-    @pl.loop(1, N_LAT)
+    @pl.loop(0, N_LAT - 1)
     def _(step):
         lat_arrival(lat_peer(step)).wait_recv()
 
@@ -223,17 +229,25 @@
         def _():
             keep_unit(16 + e, 1).start()
 
-    @pl.loop(1, N_CHAN)
+    @pl.loop(0, N_CHAN - 1)
     def _(step):
         peer = chan_peer(step)
         unit_copy(peer, 0, peer, ci).start()
 
     keep_unit(ci, 0).start()
 
-    @pl.loop(1, N_CHAN)
+    @pl.loop(0, N_CHAN - 1)
     def _(step):
         peer = chan_peer(step)
         w_copy(peer, peer).wait_recv()
+
+    @pl.loop(0, N_LAT - 1)
+    def _(step):
+        lat_copy(lat_peer(step)).wait_send()
+
+    @pl.loop(0, N_CHAN - 1)
+    def _(step):
+        w_copy(chan_peer(step), ci).wait_send()
 
     every = weights[...].astype(F32).reshape(N_CHAN, 2, CH, 128)
     w_real = every[:, 0].reshape(128, 128)
@@ -244,7 +258,7 @@
     def mix(slot, unit):
         keep_unit(unit, slot).wait()
 
-        @pl.loop(1, N_CHAN)
+        @pl.loop(0, N_CHAN - 1)
         def _(step):
             peer = chan_peer(step)
             unit_copy(unit, slot, peer, peer).wait_recv()
@@ -257,7 +271,7 @@
         imag = jnp.dot(to_imag, both, preferred_element_type=F32).reshape(N_CHAN, CH, 128)
         mixed[slot] = jnp.concatenate([real, imag], axis=1).astype(BF16)
 
-        @pl.loop(1, N_CHAN)
+        @pl.loop(0, N_CHAN - 1)
         def _(step):
             back_copy(unit, slot, chan_peer(step)).start()
 
@@ -271,7 +285,18 @@
 
     mix(0, ci)
 
-    @pl.loop(1, N_CHAN)
+    @pl.loop(0, N_CHAN - 1)
+    def _(step):
+        peer = chan_peer(step)
+        unit_copy(peer, 0, peer, ci).wait_send()
+
+    for e, owner in enumerate(EXTRA):
+
+        @pl.when(ci != owner)
+        def _():
+            unit_copy(16 + e, 1, owner, ci).wait_send()
+
+    @pl.loop(0, N_CHAN - 1)
     def _(step):
         peer = chan_peer(step)
         back_copy(peer, 0, peer).wait_recv()
@@ -293,26 +318,15 @@
             [back[k * 3 + b].astype(F32) for b in range(3)] + [last[:, k : k + 1]], axis=1
         ).astype(BF16)
 
-    @pl.loop(1, N_LAT)
-    def _(step):
-        lat_copy(lat_peer(step)).wait_send()
-
-    @pl.loop(1, N_CHAN)
-    def _(step):
-        peer = chan_peer(step)
-        w_copy(peer, ci).wait_send()
-        unit_copy(peer, 0, peer, ci).wait_send()
-        back_copy(ci, 0, peer).wait_send()
-
-    for e, owner in enumerate(EXTRA):
-
-        @pl.when(ci != owner)
-        def _():
-            unit_copy(16 + e, 1, owner, ci).wait_send()
+    @pl.loop(0, N_CHAN - 1)
+    def _(step):
+        back_copy(ci, 0, chan_peer(step)).wait_send()
+
+    for e, owner in enumerate(EXTRA):
 
         @pl.when(ci == owner)
         def _():
-            @pl.loop(1, N_CHAN)
+            @pl.loop(0, N_CHAN - 1)
             def _(step):
                 back_copy(16 + e, 1, chan_peer(step)).wait_send()
 
@@ -355,7 +369,7 @@
             dma((UNITS,)),
         ],
         compiler_params=pltpu.CompilerParams(
-            collective_id=0, has_side_effects=True, vmem_limit_bytes=48 * 1024 * 1024
+            collective_id=0, has_side_effects=True, vmem_limit_bytes=60 * 1024 * 1024
         ),
     )(
         grid_field.reshape(LAT * CH, NLON),

time: 52.1 us -> 40.1 us (0.77)
  local copies, waits for them, and re-layouts: 10.7 us -> 1.54 us
  Pallas kernels: 40.9 us -> 38.4 us
    unnamed x21 -> x1, local copies, waits for them, and re-layouts: 10.7 us -> 1.54 us
    pallas_call x1, Pallas kernels: 40.9 us -> 38.4 us  [body(): pl.pallas_call(kernel, out_shape=jax.ShapeDtypeStruct((MINE, 16, SLOTS),...]
where the time goes in v3:
time: 40.1 us; the launch traced here: 40 us
  Pallas kernels  38.4 us (96%)
  local copies, waits for them, and re-layouts  1.54 us (4%)
    pallas_call x1, Pallas kernels, body(): pl.pallas_call(kernel, out_shape=jax.ShapeDtypeStruct((MINE, 16, SLOTS),...  38.4 us
    unnamed x1, local copies, waits for them, and re-layouts  1.54 us

profile of v3, /device:TPU:1, one launch (start us, length us, event | category | flops | bytes accessed | tf_op | source)
XLA Modules:
  0.0 40.0 jit_solution(6141130557355639256)
XLA Ops:
  0.0 38.4 %shard_map.109 = bf16[6,16,385]{2,1,0:T(8,128)(2,1)} custom-call(bf16[128,1440]{1,0:T(8,128)(2,1)} %bitcast.7, bf16[6,385,512]{2,1,0:T(8,128)(2,1)} %bitcast.5, bf16[16,128]{1,0:T(8,128)(2,1)} %bitcast.8, s32[1,192]{1,0:T(1,128)} %bitcast.9, bf16[768,1440]{1,0:T(8,128)(2,1)} %constant.14.clone.table_hbm, bf16[768,192]{1,0:T(8,128)(2,1)} %constant.15.clone.pick_hbm, ...), custom_call_target="tpu_custom_call" | custom-call | tf_op jit(solution)/shard_map/pallas_call | solution.py:338
  38.4 1.5 %copy.13 = bf16[6,2,8,385]{3,2,1,0:T(8,128)(2,1)} copy(bf16[6,2,8,385]{3,2,1,0:T(8,128)(2,1)} %bitcast.6) | data formatting | bytes 147840

commit v4 on v2

v4 whole, which is shorter than its diff:
```python
import math

import jax
import jax.numpy as jnp
import ml_dtypes
import numpy as np
from jax import lax
from jax.experimental import pallas as pl
from jax.experimental.pallas import tpu as pltpu
from jax.sharding import PartitionSpec as P

BF16 = jnp.bfloat16
F32 = jnp.float32
NX, NY, NZ = 4, 8, 8
N_LAT, N_CHAN = NX * NY, 2 * NZ
LAT, CH, NLON = 16, 8, 1440
ORDERS, SLOTS, PAIRS, MINE = 384, 385, 192, 6
ROWS = 4 * MINE
UNITS = 19
APART = 5
MESH = pl.DeviceIdType.MESH
NT = (((1,), (1,)), ((), ()))


def hops(step, ring):
    return min(step, ring - step)


LAT_STEPS = sorted(
    [(dx, dy) for dx in range(NX) for dy in range(NY) if dx + dy],
    key=lambda d: -hops(d[0], NX) - hops(d[1], NY),
)
CHAN_STEPS = sorted(
    [(dz, dc) for dz in range(NZ) for dc in range(2) if dz + dc],
    key=lambda d: -2 * hops(d[0], NZ) - d[1],
)


def fourier_table():
    orders = np.arange(ORDERS, dtype=np.int32)[:, None]
    columns = np.arange(NLON, dtype=np.int32)[None, :]
    phases = np.float32(2.0 * math.pi / NLON) * ((orders * columns) % NLON).astype(np.float32)
    return np.concatenate([np.cos(phases), -np.sin(phases)], axis=0).astype(ml_dtypes.bfloat16)


def constants():
    row = np.arange(N_LAT * ROWS)
    part, half, pair = (row // 12) % 2, (row // 6) % 2, (row // ROWS) * MINE + row % MINE
    pick = np.zeros((row.size, PAIRS), np.float32)
    pick[row, pair] = 1 - 2 * half
    base = np.broadcast_to((part * ORDERS + half * (ORDERS - 1))[:, None], (row.size, 128))
    s, t, c = np.meshgrid(np.arange(8), np.arange(LAT), np.arange(CH), indexing="ij")
    regroup = np.zeros((1024, 1024), np.float32)
    regroup[(s * 128 + t * CH + c).ravel(), (c * 128 + s * LAT + t).ravel()] = 1
    lane = np.arange(CH * ROWS)
    pair_lane = np.broadcast_to((lane % MINE)[None, :], (8, lane.size))
    k, r, c = np.meshgrid(np.arange(MINE), np.arange(2), np.arange(CH), indexing="ij")
    fold = np.zeros((2, MINE * 16 + 16, CH * ROWS), np.float32)
    for half in range(2):
        fold[half, (k * 16 + r * 8 + c).ravel(), (c * ROWS + r * 12 + half * MINE + k).ravel()] = 1
    out_row = np.arange(MINE * 16)
    offset = np.arange(PAIRS)[None, :] - (out_row // 16)[:, None]
    index = np.concatenate([offset, pair_lane]).astype(np.int32)
    bf = ml_dtypes.bfloat16
    return (
        fourier_table(),
        pick.astype(bf),
        base.astype(np.float32),
        regroup.astype(bf),
        fold.astype(bf),
        index,
    )


def drain(buffer, sem):
    pltpu.make_async_copy(buffer, buffer, sem).wait()


def kernel(
    x_hbm, leg_hbm, mix_hbm, order_hbm, table_hbm, pick_hbm, base_hbm, regroup_hbm, fold_hbm, index_hbm,
    out_ref,
    x, leg, order, table, pick, base, regroup, fold, index,
    send, recv, weights, units, gathered, mixed, back,
    local_sem, lat_send, lat_recv, w_send, w_recv, c_send, c_recv, m_send, m_recv,
):
    li, ci = lax.axis_index("lat"), lax.axis_index("chan")
    loads = [
        pltpu.make_async_copy(src, dst, local_sem.at[i])
        for i, (src, dst) in enumerate(
            [
                (order_hbm, order), (pick_hbm, pick), (base_hbm, base), (x_hbm, x), (table_hbm, table),
                (mix_hbm, weights.at[ci]), (index_hbm, index), (fold_hbm, fold), (regroup_hbm, regroup),
                (leg_hbm, leg),
            ]
        )
    ]
    lx, ly, cz, cc = lax.div(li, NY), lax.rem(li, NY), lax.div(ci, 2), lax.rem(ci, 2)
    xs = [lax.rem(lx + d, NX) * NY for d in range(NX)]
    ys = [lax.rem(ly + d, NY) for d in range(NY)]
    zs = [lax.rem(cz + d, NZ) * 2 for d in range(NZ)]
    cs = [lax.rem(cc + d, 2) for d in range(2)]
    lat_peers = [xs[dx] + ys[dy] for dx, dy in LAT_STEPS]
    chan_peers = [zs[dz] + cs[dc] for dz, dc in CHAN_STEPS]

    barrier = pltpu.get_barrier_semaphore()
    for peer in lat_peers:
        pl.semaphore_signal(barrier, inc=1, device_id=(peer, ci), device_id_type=MESH)
    for peer in chan_peers:
        pl.semaphore_signal(barrier, inc=1, device_id=(li, peer), device_id_type=MESH)
    for load in loads:
        load.start()
    for load in loads[:3]:
        load.wait()
    order_rows = jnp.broadcast_to(order[...], (128, PAIRS)).astype(F32).astype(BF16)
    key = base[...] + lax.dot_general(pick[...], order_rows, NT, preferred_element_type=F32)
    column = lax.broadcasted_iota(jnp.int32, key.shape, 1).astype(F32)
    place = jnp.concatenate(
        [jnp.where(key == column + 128.0 * b, 1.0, 0.0).astype(BF16) for b in range(2 * ORDERS // 128)],
        axis=1,
    )
    for load in loads[3:5]:
        load.wait()
    spectrum = lax.dot_general(table[...], x[...], NT, preferred_element_type=F32)
    spectrum = (spectrum * (1.0 / math.sqrt(NLON))).astype(BF16)
    placed = jnp.dot(place, spectrum, preferred_element_type=F32)
    send[...] = placed.reshape(N_LAT, ROWS, 128).astype(BF16)

    pl.semaphore_wait(barrier, N_LAT + N_CHAN - 2)

    for peer in lat_peers:
        pltpu.make_async_remote_copy(
            src_ref=send.at[peer], dst_ref=recv.at[li], send_sem=lat_send.at[0], recv_sem=lat_recv.at[0],
            device_id=(peer, ci), device_id_type=MESH,
        ).start()
    pltpu.make_async_copy(send.at[li], recv.at[li], lat_recv.at[0]).start()
    loads[5].wait()
    for peer in chan_peers:
        pltpu.make_async_remote_copy(
            src_ref=weights.at[ci], dst_ref=weights.at[ci], send_sem=w_send.at[0], recv_sem=w_recv.at[0],
            device_id=(li, peer), device_id_type=MESH,
        ).start()

    for load in loads[6:]:
        load.wait()
    mine = jnp.where(index[0 : MINE * 16] == li * MINE, 1.0, 0.0).astype(BF16)
    my_order = lax.dot_general(mine, order_rows, NT, preferred_element_type=F32)
    first = lax.broadcasted_iota(jnp.int32, (MINE * 16, SLOTS), 1).astype(F32) < (
        float(ORDERS) - my_order[:, 0:1]
    )

    drain(recv, lat_recv.at[0])
    blocks = jnp.concatenate(
        [
            jnp.concatenate([recv[g * 8 + s].astype(F32) for s in range(8)], axis=1)
            for g in range(N_LAT // 8)
        ],
        axis=0,
    ).astype(BF16)
    turned = jnp.dot(blocks, regroup[...], preferred_element_type=F32)
    fields = jnp.concatenate(
        [
            jnp.concatenate(
                [turned[g * ROWS : (g + 1) * ROWS, c * 128 : (c + 1) * 128] for g in range(N_LAT // 8)],
                axis=1,
            )
            for c in range(CH)
        ],
        axis=0,
    ).astype(BF16)
    lanes = jnp.broadcast_to(index[MINE * 16 : MINE * 16 + 1], (SLOTS, CH * ROWS))
    sums = jnp.zeros((SLOTS, CH * ROWS), F32)
    for k in range(MINE):
        one = lax.dot_general(leg[k], fields, NT, preferred_element_type=F32)
        sums = jnp.where(lanes == k, one, sums)
    sums = sums.astype(BF16)
    halves = [
        lax.dot_general(fold[h, 0 : MINE * 16], sums, NT, preferred_element_type=F32) for h in range(2)
    ]
    coeffs = jnp.where(first, halves[0], halves[1])
    ends = jnp.zeros((16, 128), F32)
    end_lane = lax.broadcasted_iota(jnp.int32, (16, 128), 1)
    for k in range(MINE):
        piece = coeffs[k * 16 : (k + 1) * 16]
        for b in range(3):
            units[k * 3 + b] = piece[:, b * 128 : (b + 1) * 128].astype(BF16)
        ends = jnp.where(end_lane == k, jnp.broadcast_to(piece[:, ORDERS:], (16, 128)), ends)
    units[UNITS - 1] = ends.astype(BF16)

    def extra_copy(e):
        return pltpu.make_async_remote_copy(
            src_ref=units.at[N_CHAN + e], dst_ref=gathered.at[1, ci], send_sem=c_send.at[1 + e],
            recv_sem=c_recv.at[1], device_id=(li, e * APART), device_id_type=MESH,
        )

    def keep_unit(unit, slot):
        return pltpu.make_async_copy(units.at[unit], gathered.at[slot, ci], c_recv.at[slot])

    def send_back(unit, slot):
        for peer in chan_peers:
            pltpu.make_async_remote_copy(
                src_ref=mixed.at[slot, peer], dst_ref=back.at[unit], send_sem=m_send.at[slot],
                recv_sem=m_recv.at[0], device_id=(li, peer), device_id_type=MESH,
            ).start()
        pltpu.make_async_copy(mixed.at[slot, ci], back.at[unit], m_recv.at[0]).start()

    for peer in chan_peers:
        pltpu.make_async_remote_copy(
            src_ref=units.at[peer], dst_ref=gathered.at[0, ci], send_sem=c_send.at[0],
            recv_sem=c_recv.at[0], device_id=(li, peer), device_id_type=MESH,
        ).start()
    for e in range(UNITS - N_CHAN):

        @pl.when(ci != e * APART)
        def _():
            extra_copy(e).start()

        @pl.when(ci == e * APART)
        def _():
            keep_unit(N_CHAN + e, 1).start()

    keep_unit(ci, 0).start()

    drain(weights.at[pl.ds(0, N_CHAN - 1)], w_recv.at[0])
    every = weights[...].astype(F32).reshape(N_CHAN, 2, CH, 128)
    w_real = every[:, 0].reshape(128, 128)
    w_imag = every[:, 1].reshape(128, 128)
    to_real = jnp.concatenate([w_real, -w_imag], axis=1).astype(BF16)
    to_imag = jnp.concatenate([w_imag, w_real], axis=1).astype(BF16)
    drain(send.at[pl.ds(0, N_LAT - 1)], lat_send.at[0])
    drain(weights.at[pl.ds(0, N_CHAN - 1)], w_send.at[0])

    drain(gathered.at[0], c_recv.at[0])
    for e in range(UNITS - N_CHAN):

        @pl.when(ci == e * APART)
        def _():
            drain(gathered.at[1], c_recv.at[1])

    both = gathered[...].astype(F32).reshape(2, N_CHAN, 2, CH, 128)
    both = jnp.concatenate(
        [
            jnp.concatenate([both[slot, :, part].reshape(128, 128) for slot in range(2)], axis=1)
            for part in range(2)
        ],
        axis=0,
    ).astype(BF16)
    real = jnp.dot(to_real, both, preferred_element_type=F32)
    imag = jnp.dot(to_imag, both, preferred_element_type=F32)
    for slot in range(2):
        parts = [
            whole[:, slot * 128 : (slot + 1) * 128].reshape(N_CHAN, CH, 128) for whole in (real, imag)
        ]
        mixed[slot] = jnp.concatenate(parts, axis=1).astype(BF16)

    send_back(ci, 0)
    for e in range(UNITS - N_CHAN):

        @pl.when(ci == e * APART)
        def _():
            send_back(N_CHAN + e, 1)

    drain(units.at[pl.ds(0, N_CHAN - 1)], c_send.at[0])
    for e in range(UNITS - N_CHAN):

        @pl.when(ci != e * APART)
        def _():
            extra_copy(e).wait_send()

    drain(back, m_recv.at[0])
    last = back[UNITS - 1].astype(F32)
    for k in range(MINE):
        out_ref[k] = jnp.concatenate(
            [back[k * 3 + b].astype(F32) for b in range(3)] + [last[:, k : k + 1]], axis=1
        ).astype(BF16)

    drain(mixed.at[0, pl.ds(0, N_CHAN - 1)], m_send.at[0])
    for e in range(UNITS - N_CHAN):

        @pl.when(ci == e * APART)
        def _():
            drain(mixed.at[1, pl.ds(0, N_CHAN - 1)], m_send.at[1])


def body(grid_field, legendre, mix_weight, pair_order):
    any_spec = pl.BlockSpec(memory_space=pl.ANY)
    dma = pltpu.SemaphoreType.DMA
    fixed = [jnp.asarray(c) for c in constants()]
    out = pl.pallas_call(
        kernel,
        out_shape=jax.ShapeDtypeStruct((MINE, 16, SLOTS), BF16),
        in_specs=[any_spec] * 10,
        out_specs=pl.BlockSpec(memory_space=pltpu.VMEM),
        scratch_shapes=[
            pltpu.VMEM((LAT * CH, NLON), BF16),
            pltpu.VMEM((MINE, SLOTS, N_LAT * LAT), BF16),
            pltpu.VMEM((1, PAIRS), jnp.int32),
            pltpu.VMEM((2 * ORDERS, NLON), BF16),
            pltpu.VMEM((N_LAT * ROWS, PAIRS), BF16),
            pltpu.VMEM((N_LAT * ROWS, 128), F32),
            pltpu.VMEM((1024, 1024), BF16),
            pltpu.VMEM((2, MINE * 16 + 16, CH * ROWS), BF16),
            pltpu.VMEM((MINE * 16 + 8, PAIRS), jnp.int32),
            pltpu.VMEM((N_LAT, ROWS, 128), BF16),
            pltpu.VMEM((N_LAT, ROWS, 128), BF16),
            pltpu.VMEM((N_CHAN, 16, 128), BF16),
            pltpu.VMEM((UNITS, 16, 128), BF16),
            pltpu.VMEM((2, N_CHAN, 16, 128), BF16),
            pltpu.VMEM((2, N_CHAN, 16, 128), BF16),
            pltpu.VMEM((UNITS, 16, 128), BF16),
            dma((10,)),
            dma((1,)),
            dma((1,)),
            dma((1,)),
            dma((1,)),
            dma((1 + UNITS - N_CHAN,)),
            dma((2,)),
            dma((2,)),
            dma((1,)),
        ],
        compiler_params=pltpu.CompilerParams(
            collective_id=0, has_side_effects=True, vmem_limit_bytes=60 * 1024 * 1024
        ),
    )(
        grid_field.reshape(LAT * CH, NLON),
        jnp.transpose(legendre, (1, 2, 0)),
        mix_weight.reshape(16, 128),
        pair_order.reshape(1, PAIRS),
        *fixed,
    )
    return out.reshape(MINE, 2, CH, SLOTS)


def solution(mesh):
    return jax.shard_map(
        body,
        mesh=mesh,
        in_specs=(P("lat", "chan", None), P(None, "lat", None), P(None, "chan", None), P()),
        out_specs=P("lat", None, "chan", None),
        check_vma=False,
    )
```

time: 52.1 us -> 37.1 us (0.71)
  local copies, waits for them, and re-layouts: 10.7 us -> 1.54 us
  Pallas kernels: 40.9 us -> 35.4 us
    unnamed x21 -> x1, local copies, waits for them, and re-layouts: 10.7 us -> 1.54 us
    pallas_call x1, Pallas kernels: 40.9 us -> 35.4 us  [body(): pl.pallas_call(kernel, out_shape=jax.ShapeDtypeStruct((MINE, 16, SLOTS),...]
where the time goes in v4:
time: 37.1 us; the launch traced here: 37 us
  Pallas kernels  35.4 us (95%)
  local copies, waits for them, and re-layouts  1.54 us (4%)
    pallas_call x1, Pallas kernels, body(): pl.pallas_call(kernel, out_shape=jax.ShapeDtypeStruct((MINE, 16, SLOTS),...  35.4 us
    unnamed x1, local copies, waits for them, and re-layouts  1.54 us

profile of v4, /device:TPU:1, one launch (start us, length us, event | category | flops | bytes accessed | tf_op | source)
XLA Modules:
  0.0 37.0 jit_solution(12459193354368412942)
XLA Ops:
  0.0 35.4 %shard_map.100 = bf16[6,16,385]{2,1,0:T(8,128)(2,1)} custom-call(bf16[128,1440]{1,0:T(8,128)(2,1)} %bitcast.7, bf16[6,385,512]{2,1,0:T(8,128)(2,1)} %bitcast.5, bf16[16,128]{1,0:T(8,128)(2,1)} %bitcast.8, s32[1,192]{1,0:T(1,128)} %bitcast.9, bf16[768,1440]{1,0:T(8,128)(2,1)} %constant.12.clone.table_hbm, bf16[768,192]{1,0:T(8,128)(2,1)} %constant.13.clone.pick_hbm, ...), custom_call_target="tpu_custom_call" | custom-call | tf_op jit(solution)/shard_map/pallas_call | solution.py:288
  35.4 1.5 %copy.12 = bf16[6,2,8,385]{3,2,1,0:T(8,128)(2,1)} copy(bf16[6,2,8,385]{3,2,1,0:T(8,128)(2,1)} %bitcast.6) | data formatting | bytes 147840

commit v5 on v4

--- a/solution.py
+++ b/solution.py
@@ -287,7 +287,7 @@
     fixed = [jnp.asarray(c) for c in constants()]
     out = pl.pallas_call(
         kernel,
-        out_shape=jax.ShapeDtypeStruct((MINE, 16, SLOTS), BF16),
+        out_shape=pltpu.VMEM((MINE, 16, SLOTS), BF16),
         in_specs=[any_spec] * 10,
         out_specs=pl.BlockSpec(memory_space=pltpu.VMEM),
         scratch_shapes=[

time: 37.1 us -> 35.6 us (0.960)
  local copies, waits for them, and re-layouts: 1.54 us -> 0.64 us
  Pallas kernels: 35.4 us -> 34.8 us
    unnamed x1, local copies, waits for them, and re-layouts: 1.54 us -> 0.64 us
    pallas_call x1, Pallas kernels: 35.4 us -> 34.8 us  [body(): pl.pallas_call(kernel, out_shape=pltpu.VMEM((MINE, 16, SLOTS), BF16), in_...]
where the time goes in v5:
time: 35.6 us; the launch traced here: 35.5 us
  Pallas kernels  34.8 us (98%)
  local copies, waits for them, and re-layouts  0.64 us (2%)
    pallas_call x1, Pallas kernels, body(): pl.pallas_call(kernel, out_shape=pltpu.VMEM((MINE, 16, SLOTS), BF16), in_...  34.8 us

profile of v5, /device:TPU:1, one launch (start us, length us, event | category | flops | bytes accessed | tf_op | source)
XLA Modules:
  0.0 35.5 jit_solution(10258485935556318793)
XLA Ops:
  0.0 34.8 %shard_map.100 = bf16[6,16,385]{2,1,0:T(8,128)(2,1)S(1)} custom-call(bf16[128,1440]{1,0:T(8,128)(2,1)} %bitcast.7, bf16[6,385,512]{2,1,0:T(8,128)(2,1)} %bitcast.6, bf16[16,128]{1,0:T(8,128)(2,1)} %bitcast.8, s32[1,192]{1,0:T(1,128)} %bitcast.9, bf16[768,1440]{1,0:T(8,128)(2,1)} %constant.12.clone.table_hbm, bf16[768,192]{1,0:T(8,128)(2,1)} %constant.13.clone.pick_hbm, ...), custom_call_target="tpu_custom_call" | custom-call | tf_op jit(solution)/shard_map/pallas_call | solution.py:288
  34.8 0.6 %copy.12 = bf16[6,2,8,385]{3,2,1,0:T(8,128)(2,1)} copy(bf16[6,2,8,385]{3,2,1,0:T(8,128)(2,1)S(1)} %bitcast.5) | data formatting | bytes 147840

commit v6 on v5

--- a/solution.py
+++ b/solution.py
@@ -52,22 +52,20 @@
     s, t, c = np.meshgrid(np.arange(8), np.arange(LAT), np.arange(CH), indexing="ij")
     regroup = np.zeros((1024, 1024), np.float32)
     regroup[(s * 128 + t * CH + c).ravel(), (c * 128 + s * LAT + t).ravel()] = 1
-    lane = np.arange(CH * ROWS)
-    pair_lane = np.broadcast_to((lane % MINE)[None, :], (8, lane.size))
     k, r, c = np.meshgrid(np.arange(MINE), np.arange(2), np.arange(CH), indexing="ij")
-    fold = np.zeros((2, MINE * 16 + 16, CH * ROWS), np.float32)
+    arrange = np.zeros((CH * ROWS, CH * ROWS), np.float32)
     for half in range(2):
-        fold[half, (k * 16 + r * 8 + c).ravel(), (c * ROWS + r * 12 + half * MINE + k).ravel()] = 1
+        arrange[(k * 32 + half * 16 + r * 8 + c).ravel(), (c * ROWS + r * 12 + half * MINE + k).ravel()] = 1
     out_row = np.arange(MINE * 16)
     offset = np.arange(PAIRS)[None, :] - (out_row // 16)[:, None]
-    index = np.concatenate([offset, pair_lane]).astype(np.int32)
+    index = offset.astype(np.int32)
     bf = ml_dtypes.bfloat16
     return (
         fourier_table(),
         pick.astype(bf),
         base.astype(np.float32),
         regroup.astype(bf),
-        fold.astype(bf),
+        arrange.astype(bf),
         index,
     )
 
@@ -77,9 +75,9 @@
 
 
 def kernel(
-    x_hbm, leg_hbm, mix_hbm, order_hbm, table_hbm, pick_hbm, base_hbm, regroup_hbm, fold_hbm, index_hbm,
+    x_hbm, leg_hbm, mix_hbm, order_hbm, table_hbm, pick_hbm, base_hbm, regroup_hbm, arrange_hbm, index_hbm,
     out_ref,
-    x, leg, order, table, pick, base, regroup, fold, index,
+    x, leg, order, table, pick, base, regroup, arrange, index,
     send, recv, weights, units, gathered, mixed, back,
     local_sem, lat_send, lat_recv, w_send, w_recv, c_send, c_recv, m_send, m_recv,
 ):
@@ -88,9 +86,9 @@
         pltpu.make_async_copy(src, dst, local_sem.at[i])
         for i, (src, dst) in enumerate(
             [
-                (order_hbm, order), (pick_hbm, pick), (base_hbm, base), (x_hbm, x), (table_hbm, table),
-                (mix_hbm, weights.at[ci]), (index_hbm, index), (fold_hbm, fold), (regroup_hbm, regroup),
-                (leg_hbm, leg),
+                (order_hbm, order), (pick_hbm, pick), (base_hbm, base), (x_hbm, x), (table_hbm.at[pl.ds(0, ORDERS)], table.at[pl.ds(0, ORDERS)]),
+                (mix_hbm, weights.at[ci]), (index_hbm, index), (arrange_hbm, arrange), (regroup_hbm, regroup),
+                (leg_hbm, leg), (table_hbm.at[pl.ds(ORDERS, ORDERS)], table.at[pl.ds(ORDERS, ORDERS)]),
             ]
         )
     ]
@@ -102,12 +100,14 @@
     lat_peers = [xs[dx] + ys[dy] for dx, dy in LAT_STEPS]
     chan_peers = [zs[dz] + cs[dc] for dz, dc in CHAN_STEPS]
 
+    for load in loads[:5]:
+        load.start()
     barrier = pltpu.get_barrier_semaphore()
     for peer in lat_peers:
         pl.semaphore_signal(barrier, inc=1, device_id=(peer, ci), device_id_type=MESH)
     for peer in chan_peers:
         pl.semaphore_signal(barrier, inc=1, device_id=(li, peer), device_id_type=MESH)
-    for load in loads:
+    for load in loads[10:] + loads[5:10]:
         load.start()
     for load in loads[:3]:
         load.wait()
@@ -118,11 +118,14 @@
         [jnp.where(key == column + 128.0 * b, 1.0, 0.0).astype(BF16) for b in range(2 * ORDERS // 128)],
         axis=1,
     )
-    for load in loads[3:5]:
+    loads[3].wait()
+    parts = []
+    for load, part in ((loads[4], 0), (loads[10], 1)):
         load.wait()
-    spectrum = lax.dot_general(table[...], x[...], NT, preferred_element_type=F32)
-    spectrum = (spectrum * (1.0 / math.sqrt(NLON))).astype(BF16)
-    placed = jnp.dot(place, spectrum, preferred_element_type=F32)
+        rows = table[part * ORDERS : (part + 1) * ORDERS]
+        spectrum = lax.dot_general(rows, x[...], NT, preferred_element_type=F32)
+        parts.append((spectrum * (1.0 / math.sqrt(NLON))).astype(BF16))
+    placed = jnp.dot(place, jnp.concatenate(parts, axis=0), preferred_element_type=F32)
     send[...] = placed.reshape(N_LAT, ROWS, 128).astype(BF16)
 
     pl.semaphore_wait(barrier, N_LAT + N_CHAN - 2)
@@ -140,9 +143,9 @@
             device_id=(li, peer), device_id_type=MESH,
         ).start()
 
-    for load in loads[6:]:
+    for load in loads[6:10]:
         load.wait()
-    mine = jnp.where(index[0 : MINE * 16] == li * MINE, 1.0, 0.0).astype(BF16)
+    mine = jnp.where(index[...] == li * MINE, 1.0, 0.0).astype(BF16)
     my_order = lax.dot_general(mine, order_rows, NT, preferred_element_type=F32)
     first = lax.broadcasted_iota(jnp.int32, (MINE * 16, SLOTS), 1).astype(F32) < (
         float(ORDERS) - my_order[:, 0:1]
@@ -167,20 +170,14 @@
         ],
         axis=0,
     ).astype(BF16)
-    lanes = jnp.broadcast_to(index[MINE * 16 : MINE * 16 + 1], (SLOTS, CH * ROWS))
-    sums = jnp.zeros((SLOTS, CH * ROWS), F32)
-    for k in range(MINE):
-        one = lax.dot_general(leg[k], fields, NT, preferred_element_type=F32)
-        sums = jnp.where(lanes == k, one, sums)
-    sums = sums.astype(BF16)
-    halves = [
-        lax.dot_general(fold[h, 0 : MINE * 16], sums, NT, preferred_element_type=F32) for h in range(2)
-    ]
-    coeffs = jnp.where(first, halves[0], halves[1])
+    fields = jnp.dot(arrange[...], fields, preferred_element_type=F32).astype(BF16)
     ends = jnp.zeros((16, 128), F32)
     end_lane = lax.broadcasted_iota(jnp.int32, (16, 128), 1)
     for k in range(MINE):
-        piece = coeffs[k * 16 : (k + 1) * 16]
+        sums = lax.dot_general(
+            fields[k * 32 : (k + 1) * 32], leg[k], NT, preferred_element_type=F32
+        )
+        piece = jnp.where(first[k * 16 : (k + 1) * 16], sums[0:16], sums[16:32])
         for b in range(3):
             units[k * 3 + b] = piece[:, b * 128 : (b + 1) * 128].astype(BF16)
         ends = jnp.where(end_lane == k, jnp.broadcast_to(piece[:, ORDERS:], (16, 128)), ends)
@@ -298,8 +295,8 @@
             pltpu.VMEM((N_LAT * ROWS, PAIRS), BF16),
             pltpu.VMEM((N_LAT * ROWS, 128), F32),
             pltpu.VMEM((1024, 1024), BF16),
-            pltpu.VMEM((2, MINE * 16 + 16, CH * ROWS), BF16),
-            pltpu.VMEM((MINE * 16 + 8, PAIRS), jnp.int32),
+            pltpu.VMEM((CH * ROWS, CH * ROWS), BF16),
+            pltpu.VMEM((MINE * 16, PAIRS), jnp.int32),
             pltpu.VMEM((N_LAT, ROWS, 128), BF16),
             pltpu.VMEM((N_LAT, ROWS, 128), BF16),
             pltpu.VMEM((N_CHAN, 16, 128), BF16),
@@ -307,7 +304,7 @@
             pltpu.VMEM((2, N_CHAN, 16, 128), BF16),
             pltpu.VMEM((2, N_CHAN, 16, 128), BF16),
             pltpu.VMEM((UNITS, 16, 128), BF16),
-            dma((10,)),
+            dma((11,)),
             dma((1,)),
             dma((1,)),
             dma((1,)),

time: 35.6 us -> 34.6 us (0.972)
  Pallas kernels: 34.8 us -> 33.8 us
    pallas_call x1, Pallas kernels: 34.8 us -> 33.8 us  [body(): pl.pallas_call(kernel, out_shape=pltpu.VMEM((MINE, 16, SLOTS), BF16), in_...]
where the time goes in v6:
time: 34.6 us; the launch traced here: 34.5 us
  Pallas kernels  33.8 us (98%)
  local copies, waits for them, and re-layouts  0.64 us (2%)
    pallas_call x1, Pallas kernels, body(): pl.pallas_call(kernel, out_shape=pltpu.VMEM((MINE, 16, SLOTS), BF16), in_...  33.8 us

profile of v6, /device:TPU:1, one launch (start us, length us, event | category | flops | bytes accessed | tf_op | source)
XLA Modules:
  0.0 34.5 jit_solution(14448502197048119251)
XLA Ops:
  0.0 33.8 %shard_map.100 = bf16[6,16,385]{2,1,0:T(8,128)(2,1)S(1)} custom-call(bf16[128,1440]{1,0:T(8,128)(2,1)} %bitcast.7, bf16[6,385,512]{2,1,0:T(8,128)(2,1)} %bitcast.6, bf16[16,128]{1,0:T(8,128)(2,1)} %bitcast.8, s32[1,192]{1,0:T(1,128)} %bitcast.9, bf16[768,1440]{1,0:T(8,128)(2,1)} %constant.12.clone.table_hbm, bf16[768,192]{1,0:T(8,128)(2,1)} %constant.13.clone.pick_hbm, ...), custom_call_target="tpu_custom_call" | custom-call | tf_op jit(solution)/shard_map/pallas_call | solution.py:285
  33.8 0.6 %copy.12 = bf16[6,2,8,385]{3,2,1,0:T(8,128)(2,1)} copy(bf16[6,2,8,385]{3,2,1,0:T(8,128)(2,1)S(1)} %bitcast.5) | data formatting | bytes 147840

commit v7 on v6

--- a/solution.py
+++ b/solution.py
@@ -77,7 +77,7 @@
 def kernel(
     x_hbm, leg_hbm, mix_hbm, order_hbm, table_hbm, pick_hbm, base_hbm, regroup_hbm, arrange_hbm, index_hbm,
     out_ref,
-    x, leg, order, table, pick, base, regroup, arrange, index,
+    x, leg, turned_leg, order, table, pick, base, regroup, arrange, index,
     send, recv, weights, units, gathered, mixed, back,
     local_sem, lat_send, lat_recv, w_send, w_recv, c_send, c_recv, m_send, m_recv,
 ):
@@ -103,10 +103,10 @@
     for load in loads[:5]:
         load.start()
     barrier = pltpu.get_barrier_semaphore()
-    for peer in lat_peers:
-        pl.semaphore_signal(barrier, inc=1, device_id=(peer, ci), device_id_type=MESH)
-    for peer in chan_peers:
-        pl.semaphore_signal(barrier, inc=1, device_id=(li, peer), device_id_type=MESH)
+    far = [(hops(dx, NX) + hops(dy, NY), peer, ci) for (dx, dy), peer in zip(LAT_STEPS, lat_peers)]
+    far += [(hops(dz, NZ), li, peer) for (dz, dc), peer in zip(CHAN_STEPS, chan_peers)]
+    for _, lat, chan in sorted(far, key=lambda f: -f[0]):
+        pl.semaphore_signal(barrier, inc=1, device_id=(lat, chan), device_id_type=MESH)
     for load in loads[10:] + loads[5:10]:
         load.start()
     for load in loads[:3]:
@@ -150,6 +150,11 @@
     first = lax.broadcasted_iota(jnp.int32, (MINE * 16, SLOTS), 1).astype(F32) < (
         float(ORDERS) - my_order[:, 0:1]
     )
+
+    lat_ids = [lax.broadcasted_iota(jnp.int32, (N_LAT * LAT, N_LAT * LAT), d) for d in range(2)]
+    unit = jnp.where(lat_ids[0] == lat_ids[1], 1.0, 0.0).astype(BF16)
+    for k in range(MINE):
+        turned_leg[k] = lax.dot_general(unit, leg[k], NT, preferred_element_type=F32).astype(BF16)
 
     drain(recv, lat_recv.at[0])
     blocks = jnp.concatenate(
@@ -174,9 +179,7 @@
     ends = jnp.zeros((16, 128), F32)
     end_lane = lax.broadcasted_iota(jnp.int32, (16, 128), 1)
     for k in range(MINE):
-        sums = lax.dot_general(
-            fields[k * 32 : (k + 1) * 32], leg[k], NT, preferred_element_type=F32
-        )
+        sums = jnp.dot(fields[k * 32 : (k + 1) * 32], turned_leg[k], preferred_element_type=F32)
         piece = jnp.where(first[k * 16 : (k + 1) * 16], sums[0:16], sums[16:32])
         for b in range(3):
             units[k * 3 + b] = piece[:, b * 128 : (b + 1) * 128].astype(BF16)
@@ -290,6 +293,7 @@
         scratch_shapes=[
             pltpu.VMEM((LAT * CH, NLON), BF16),
             pltpu.VMEM((MINE, SLOTS, N_LAT * LAT), BF16),
+            pltpu.VMEM((MINE, N_LAT * LAT, SLOTS), BF16),
             pltpu.VMEM((1, PAIRS), jnp.int32),
             pltpu.VMEM((2 * ORDERS, NLON), BF16),
             pltpu.VMEM((N_LAT * ROWS, PAIRS), BF16),

time: 34.6 us -> 34.5 us (level)
  no operation moved by 1% of the time
where the time goes in v7:
time: 34.5 us; the launch traced here: 34.4 us
  Pallas kernels  33.8 us (98%)
  local copies, waits for them, and re-layouts  0.64 us (2%)
    pallas_call x1, Pallas kernels, body(): pl.pallas_call(kernel, out_shape=pltpu.VMEM((MINE, 16, SLOTS), BF16), in_...  33.8 us

profile of v7, /device:TPU:1, one launch (start us, length us, event | category | flops | bytes accessed | tf_op | source)
XLA Modules:
  0.0 34.4 jit_solution(13750439585371012890)
XLA Ops:
  0.0 33.8 %shard_map.100 = bf16[6,16,385]{2,1,0:T(8,128)(2,1)S(1)} custom-call(bf16[128,1440]{1,0:T(8,128)(2,1)} %bitcast.7, bf16[6,385,512]{2,1,0:T(8,128)(2,1)} %bitcast.6, bf16[16,128]{1,0:T(8,128)(2,1)} %bitcast.8, s32[1,192]{1,0:T(1,128)} %bitcast.9, bf16[768,1440]{1,0:T(8,128)(2,1)} %constant.12.clone.table_hbm, bf16[768,192]{1,0:T(8,128)(2,1)} %constant.13.clone.pick_hbm, ...), custom_call_target="tpu_custom_call" | custom-call | tf_op jit(solution)/shard_map/pallas_call | solution.py:288
  33.8 0.6 %copy.12 = bf16[6,2,8,385]{3,2,1,0:T(8,128)(2,1)} copy(bf16[6,2,8,385]{3,2,1,0:T(8,128)(2,1)S(1)} %bitcast.5) | data formatting | bytes 147840

commit v8 on v7

--- a/solution.py
+++ b/solution.py
@@ -203,21 +203,21 @@
             ).start()
         pltpu.make_async_copy(mixed.at[slot, ci], back.at[unit], m_recv.at[0]).start()
 
+    for e in range(UNITS - N_CHAN):
+
+        @pl.when(ci != e * APART)
+        def _():
+            extra_copy(e).start()
+
+        @pl.when(ci == e * APART)
+        def _():
+            keep_unit(N_CHAN + e, 1).start()
+
     for peer in chan_peers:
         pltpu.make_async_remote_copy(
             src_ref=units.at[peer], dst_ref=gathered.at[0, ci], send_sem=c_send.at[0],
             recv_sem=c_recv.at[0], device_id=(li, peer), device_id_type=MESH,
         ).start()
-    for e in range(UNITS - N_CHAN):
-
-        @pl.when(ci != e * APART)
-        def _():
-            extra_copy(e).start()
-
-        @pl.when(ci == e * APART)
-        def _():
-            keep_unit(N_CHAN + e, 1).start()
-
     keep_unit(ci, 0).start()
 
     drain(weights.at[pl.ds(0, N_CHAN - 1)], w_recv.at[0])

time: 34.5 us -> 34.2 us (level)
  no operation moved by 1% of the time
where the time goes in v8:
time: 34.2 us; the launch traced here: 34.1 us
  Pallas kernels  33.5 us (98%)
  local copies, waits for them, and re-layouts  0.64 us (2%)
    pallas_call x1, Pallas kernels, body(): pl.pallas_call(kernel, out_shape=pltpu.VMEM((MINE, 16, SLOTS), BF16), in_...  33.5 us

profile of v8, /device:TPU:1, one launch (start us, length us, event | category | flops | bytes accessed | tf_op | source)
XLA Modules:
  0.0 34.1 jit_solution(13587023616231030400)
XLA Ops:
  0.0 33.5 %shard_map.100 = bf16[6,16,385]{2,1,0:T(8,128)(2,1)S(1)} custom-call(bf16[128,1440]{1,0:T(8,128)(2,1)} %bitcast.7, bf16[6,385,512]{2,1,0:T(8,128)(2,1)} %bitcast.6, bf16[16,128]{1,0:T(8,128)(2,1)} %bitcast.8, s32[1,192]{1,0:T(1,128)} %bitcast.9, bf16[768,1440]{1,0:T(8,128)(2,1)} %constant.12.clone.table_hbm, bf16[768,192]{1,0:T(8,128)(2,1)} %constant.13.clone.pick_hbm, ...), custom_call_target="tpu_custom_call" | custom-call | tf_op jit(solution)/shard_map/pallas_call | solution.py:288
  33.5 0.6 %copy.12 = bf16[6,2,8,385]{3,2,1,0:T(8,128)(2,1)} copy(bf16[6,2,8,385]{3,2,1,0:T(8,128)(2,1)S(1)} %bitcast.5) | data formatting | bytes 147840

commit v9 on v8

--- a/solution.py
+++ b/solution.py
@@ -252,12 +252,13 @@
         ]
         mixed[slot] = jnp.concatenate(parts, axis=1).astype(BF16)
 
+    for e in range(UNITS - N_CHAN):
+
+        @pl.when(ci == e * APART)
+        def _():
+            send_back(N_CHAN + e, 1)
+
     send_back(ci, 0)
-    for e in range(UNITS - N_CHAN):
-
-        @pl.when(ci == e * APART)
-        def _():
-            send_back(N_CHAN + e, 1)
 
     drain(units.at[pl.ds(0, N_CHAN - 1)], c_send.at[0])
     for e in range(UNITS - N_CHAN):

time: 34.2 us -> 34.2 us (level)
  no operation moved by 1% of the time
where the time goes in v9:
time: 34.2 us; the launch traced here: 34.1 us
  Pallas kernels  33.5 us (98%)
  local copies, waits for them, and re-layouts  0.64 us (2%)
    pallas_call x1, Pallas kernels, body(): pl.pallas_call(kernel, out_shape=pltpu.VMEM((MINE, 16, SLOTS), BF16), in_...  33.5 us

profile of v9, /device:TPU:1, one launch (start us, length us, event | category | flops | bytes accessed | tf_op | source)
XLA Modules:
  0.0 34.1 jit_solution(11836593865682030475)
XLA Ops:
  0.0 33.5 %shard_map.100 = bf16[6,16,385]{2,1,0:T(8,128)(2,1)S(1)} custom-call(bf16[128,1440]{1,0:T(8,128)(2,1)} %bitcast.7, bf16[6,385,512]{2,1,0:T(8,128)(2,1)} %bitcast.6, bf16[16,128]{1,0:T(8,128)(2,1)} %bitcast.8, s32[1,192]{1,0:T(1,128)} %bitcast.9, bf16[768,1440]{1,0:T(8,128)(2,1)} %constant.12.clone.table_hbm, bf16[768,192]{1,0:T(8,128)(2,1)} %constant.13.clone.pick_hbm, ...), custom_call_target="tpu_custom_call" | custom-call | tf_op jit(solution)/shard_map/pallas_call | solution.py:289
  33.5 0.6 %copy.12 = bf16[6,2,8,385]{3,2,1,0:T(8,128)(2,1)} copy(bf16[6,2,8,385]{3,2,1,0:T(8,128)(2,1)S(1)} %bitcast.5) | data formatting | bytes 147840
